TPU v7x, 256 devices: a whole 4x4x8 slice. The times are simulated.
256 devices in a mesh: lon: 32 (over y_lo, z, core), lat: 8 (over x, y_hi).
Axes of the slice: x: 4, y: 4 (y_hi: 2, y_lo: 2; y = y_hi * 2 + y_lo), z: 8, core: 2. Of those that a mesh axis runs over, the one named last changes fastest.
Arguments:
- heat_content: float32 [16, 1024, 4096], P(None, 'lat', 'lon'), may hold values from -18 to 18
- eastern_current: float32 [16, 1024, 4096], P(None, 'lat', 'lon'), may hold values from -12 to 12
- northern_current: float32 [16, 1024, 4096], P(None, 'lat', 'lon'), may hold values from -12 to 12
- mixing_coefficient: float32 [16, 1024, 4096], P(None, 'lat', 'lon'), may hold values from 0.1 to 1
- friction_coefficient: float32 [1024, 4096], P('lat', 'lon'), may hold values from 0.05 to 0.5
- water_indicator: int32 [1024, 4096], P('lat', 'lon'), may hold values from 0 to 1
- flooded_strata: int32 [1024, 4096], P('lat', 'lon'), may hold values from 12 to 16
Outputs:
- temp_next: float32 [16, 1024, 4096], P(None, 'lat', 'lon')
- u_next: float32 [16, 1024, 4096], P(None, 'lat', 'lon')
- v_next: float32 [16, 1024, 4096], P(None, 'lat', 'lon')
All inputs are finite; a program needn't handle non-finite values.
Results may differ from a plain program's by a relative error of at most 0.0003.
Values sent between devices are 32-bit elements; how exact they have to be, the bound alone decides.
A program may use at most 128 MiB of HBM per device.

v0:
```python
import jax
import jax.numpy as jnp
from jax import lax
from jax.sharding import PartitionSpec as P

DT = 0.25
GRAV = 0.1


def extended_2(x, sides, width, wrap):
    for axis, dim in sides:
        peers, length = (lax.axis_size(axis), x.shape[dim])
        up = [(i, (i + 1) % peers) for i in range(peers if wrap else peers - 1)]
        down = [(j, i) for i, j in up]
        last = lax.slice_in_dim(x, length - width, length, axis=dim)
        first = lax.slice_in_dim(x, 0, width, axis=dim)
        before = lax.ppermute(last, axis, up)
        after = lax.ppermute(first, axis, down)
        x = jnp.concatenate([before, x, after], axis=dim)
    return x


def partner(block, axis, stride):
    count = lax.axis_size(axis)
    route = []
    for low in range(count):
        high = low | 1 << stride
        if high != low and high < count:
            route += [(low, high), (high, low)]
    return lax.ppermute(block, axis, route)


def wet_mask(stratum_plane, stratum_number):
    level_index = jnp.arange(stratum_number, dtype=jnp.float32)[:, None, None]
    return (level_index < stratum_plane[None]).astype(jnp.float32)


def neighbours(field):
    return (
        field[:, 1:-1, 1:-1],
        field[:, 1:-1, 2:],
        field[:, 1:-1, :-2],
        field[:, 2:, 1:-1],
        field[:, :-2, 1:-1],
    )


def tracer_step(tracer, u_field, v_field, diffus, wetness):
    t_mid, t_east, t_west, t_north, t_south = neighbours(tracer)
    u_mid, u_east, u_west, u_north, u_south = neighbours(u_field)
    v_mid, v_east, v_west, v_north, v_south = neighbours(v_field)
    k_mid, k_east, k_west, k_north, k_south = neighbours(diffus)
    w_mid, w_east, w_west, w_north, w_south = neighbours(wetness)
    flux_east = (
        w_mid
        * w_east
        * (0.25 * (u_mid + u_east) * (t_mid + t_east) - 0.5 * (k_mid + k_east) * (t_east - t_mid))
    )
    flux_west = (
        w_mid
        * w_west
        * (0.25 * (u_west + u_mid) * (t_west + t_mid) - 0.5 * (k_west + k_mid) * (t_mid - t_west))
    )
    flux_north = (
        w_mid
        * w_north
        * (
            0.25 * (v_mid + v_north) * (t_mid + t_north)
            - 0.5 * (k_mid + k_north) * (t_north - t_mid)
        )
    )
    flux_south = (
        w_mid
        * w_south
        * (
            0.25 * (v_south + v_mid) * (t_south + t_mid)
            - 0.5 * (k_south + k_mid) * (t_mid - t_south)
        )
    )
    flux_up = w_mid[1:] * w_mid[:-1] * 0.5 * (k_mid[1:] + k_mid[:-1]) * (t_mid[1:] - t_mid[:-1])
    zero_level = jnp.zeros_like(t_mid[:1])
    vertical = jnp.concatenate([flux_up, zero_level], 0) - jnp.concatenate([zero_level, flux_up], 0)
    return w_mid * (t_mid + DT * (flux_west - flux_east + flux_south - flux_north + vertical))


def laplace(field, wetness):
    f_mid, f_east, f_west, f_north, f_south = neighbours(field)
    w_mid, w_east, w_west, w_north, w_south = neighbours(wetness)
    return w_mid * (
        w_east * (f_east - f_mid)
        + w_west * (f_west - f_mid)
        + w_north * (f_north - f_mid)
        + w_south * (f_south - f_mid)
    )


def momentum_step(u_field, v_field, pressure, wetness, friction_coefficient, coriolis):
    p_mid, p_east, p_west, p_north, p_south = neighbours(pressure)
    w_mid = wetness[:, 1:-1, 1:-1]
    u_mid = u_field[:, 1:-1, 1:-1]
    v_mid = v_field[:, 1:-1, 1:-1]
    u_new = w_mid * (
        u_mid
        + DT
        * (
            coriolis * v_mid
            - GRAV * 0.5 * (p_east - p_west)
            + friction_coefficient * laplace(u_field, wetness)
        )
    )
    v_new = w_mid * (
        v_mid
        + DT
        * (
            -coriolis * u_mid
            - GRAV * 0.5 * (p_north - p_south)
            + friction_coefficient * laplace(v_field, wetness)
        )
    )
    return (u_new, v_new)


def extend(layered_fields, margin, plane_signs):
    parallel_summed = layered_fields.shape[1]
    lon_wide = extended_2(layered_fields, (("lon", 2),), margin, True)
    both_wide = extended_2(lon_wide, (("lat", 1),), margin, False)
    mirror = both_wide[:, parallel_summed : parallel_summed + margin, :]
    for bit_index in range(lax.axis_size("lon").bit_length() - 1):
        mirror = partner(mirror, "lon", bit_index)
    mirror = mirror[:, ::-1, ::-1]
    mirror = mirror * plane_signs[:, None, None]
    is_top = lax.axis_index("lat") == lax.axis_size("lat") - 1
    north_rows = jnp.where(is_top, mirror, both_wide[:, parallel_summed + margin :, :])
    return jnp.concatenate([both_wide[:, : parallel_summed + margin, :], north_rows], 1)


def on_device(
    heat_content,
    eastern_current,
    northern_current,
    mixing_coefficient,
    friction_coefficient,
    water_indicator,
    flooded_strata,
):
    stratum_number, parallel_summed, stack_summed = heat_content.shape
    stratum_plane = (water_indicator * flooded_strata).astype(jnp.float32)[None]
    layered_fields = jnp.concatenate(
        [heat_content, eastern_current, northern_current, mixing_coefficient, stratum_plane], 0
    )
    plane_signs = jnp.concatenate(
        [
            jnp.ones((stratum_number,), jnp.float32),
            -jnp.ones((2 * stratum_number,), jnp.float32),
            jnp.ones((stratum_number + 1,), jnp.float32),
        ]
    )
    lat_start = (lax.axis_index("lat") * parallel_summed).astype(jnp.float32)
    row_global = jnp.arange(parallel_summed, dtype=jnp.float32) + lat_start
    coriolis = jnp.sin(
        jnp.pi * ((row_global + 0.5) / (parallel_summed * lax.axis_size("lat")) - 0.5)
    )[:, None]
    extended = extend(layered_fields, 1, plane_signs)
    scalar_bordered = extended[:stratum_number]
    u_wide = extended[stratum_number : 2 * stratum_number]
    v_wide = extended[2 * stratum_number : 3 * stratum_number]
    k_wide = extended[3 * stratum_number : 4 * stratum_number]
    wetness = wet_mask(extended[4 * stratum_number], stratum_number)
    temp_next = tracer_step(scalar_bordered, u_wide, v_wide, k_wide, wetness)
    pressure = jnp.cumsum(temp_next, axis=0)
    p_wide = extend(pressure, 1, jnp.ones((stratum_number,), jnp.float32))
    u_next, v_next = momentum_step(u_wide, v_wide, p_wide, wetness, friction_coefficient, coriolis)
    return (temp_next, u_next, v_next)


def solution(mesh):
    return jax.shard_map(
        on_device,
        mesh=mesh,
        in_specs=(
            P(None, "lat", "lon"),
            P(None, "lat", "lon"),
            P(None, "lat", "lon"),
            P(None, "lat", "lon"),
            P("lat", "lon"),
            P("lat", "lon"),
            P("lat", "lon"),
        ),
        out_specs=(P(None, "lat", "lon"), P(None, "lat", "lon"), P(None, "lat", "lon")),
        check_vma=False,
    )
```

profile of v0, /device:TPU:6, one launch (start us, length us, event | category | flops | bytes accessed | tf_op | source)
XLA Modules:
  0.0 137.1 jit_solution(6859286715894716039)
XLA Ops:
  0.7 1.4 %constant_dynamic-update-slice_fusion.3 = f32[65,128,128]{2,1,0:T(8,128)S(1)} fusion(f32[16,128,128]{2,1,0:T(8,128)} %param.7), kind=kLoop, calls=%fused_computation.105 | loop fusion | bytes 2097152
  2.1 1.3 constant_dynamic-update-slice_fusion.2
  3.7 4.9 %fusion.60 = (f32[65,128,1]{2,1,0:T(8,128)}, f32[65,128,1]{2,1,0:T(8,128)}) fusion(f32[65,128,128]{2,1,0:T(8,128)S(1)} %bitcast_dynamic-update-slice_fusion), kind=kLoop, calls=%fused_computation.108 | loop fusion | bytes 133120 | tf_op jit(solution)/shard_map/slice | solution.py:15
  8.6 2.9 %copy.10 = f32[65,128,1]{1,2,0:T(1,128)S(1)} copy(f32[65,128,1]{2,1,0:T(8,128)} %get-tuple-element.5) | data formatting | bytes 66560 | tf_op jit(solution)/shard_map/slice | solution.py:15
  11.6 2.9 %copy.11 = f32[65,128,1]{1,2,0:T(1,128)S(1)} copy(f32[65,128,1]{2,1,0:T(8,128)} %get-tuple-element.6) | data formatting | bytes 66560 | tf_op jit(solution)/shard_map/slice | solution.py:16
  14.6 6.4 %collective-permute-start.1 = (f32[65,128,1]{1,2,0:T(1,128)S(1)}, f32[65,128,1]{1,2,0:T(1,128)S(1)}, u32[]{:S(2)}, u32[]{:S(2)}) collective-permute-start(f32[65,128,1]{1,2,0:T(1,128)S(1)} %copy.11), channel_id=1, source_target_pairs={{8,0},{16,8},{24,16},{32,24},{40,32},{48,40},{56,48},{64,56},{72,6... | collective-permute-start | bytes 99848 | tf_op jit(solution)/shard_map/ppermute | solution.py:18
  20.9 2.8 %copy.12 = f32[65,128,1]{2,1,0:T(8,128)} copy(f32[65,128,1]{1,2,0:T(1,128)S(1)} %collective-permute-done) | data formatting | bytes 66560 | tf_op jit(solution)/shard_map/ppermute | solution.py:17
  23.8 2.8 %copy.13 = f32[65,128,1]{2,1,0:T(8,128)} copy(f32[65,128,1]{1,2,0:T(1,128)S(1)} %collective-permute-done.1) | data formatting | bytes 66560 | tf_op jit(solution)/shard_map/ppermute | solution.py:18
  26.6 1.9 %pad_maximum_fusion.30 = (f32[65,1,130]{2,1,0:T(1,128)S(1)}, f32[65,1,130]{2,1,0:T(1,128)S(1)}) fusion(f32[65,128,1]{2,1,0:T(8,128)} %copy.13, f32[65,128,128]{2,1,0:T(8,128)} %copy-done, f32[65,128,1]{2,1,0:T(8,128)} %copy.12), kind=kLoop, calls=%fused_computation.96 | loop fusion | flops 33800 | bytes 4394000 | tf_op jit(solution)/shard_map/slice | solution.py:15
  28.5 0.1 collective-permute-start.3
  28.6 1.2 collective-permute-done.3
  29.8 4.3 %collective-permute-done.4 = f32[65,1,130]{2,1,0:T(1,128)S(1)} collective-permute-done((f32[65,1,130]{2,1,0:T(1,128)S(1)}, f32[65,1,130]{2,1,0:T(1,128)S(1)}, u32[]{:S(2)}, u32[]{:S(2)}) %collective-permute-start.4) | collective-permute-done | bytes 33832 | tf_op jit(solution)/shard_map/ppermute | solution.py:30
  34.1 1.8 %collective-permute-start.5 = (f32[65,1,130]{2,1,0:T(1,128)S(1)}, f32[65,1,130]{2,1,0:T(1,128)S(1)}, u32[]{:S(2)}, u32[]{:S(2)}) collective-permute-start(f32[65,1,130]{2,1,0:T(1,128)S(1)} %collective-permute-done.4), channel_id=1, source_target_pairs={{0,32},{32,0},{8,40},{40,8},{16,48},{48,16},{24,56},{56,24},{64,96... | collective-permute-start | bytes 101408 | tf_op jit(solution)/shard_map/ppermute | solution.py:30
  35.9 4.1 %collective-permute-done.5 = f32[65,1,130]{2,1,0:T(1,128)S(1)} collective-permute-done((f32[65,1,130]{2,1,0:T(1,128)S(1)}, f32[65,1,130]{2,1,0:T(1,128)S(1)}, u32[]{:S(2)}, u32[]{:S(2)}) %collective-permute-start.5) | collective-permute-done | bytes 33832 | tf_op jit(solution)/shard_map/ppermute | solution.py:30
  40.0 3.4 %collective-permute-start.6 = (f32[65,1,130]{2,1,0:T(1,128)S(1)}, f32[65,1,130]{2,1,0:T(1,128)S(1)}, u32[]{:S(2)}, u32[]{:S(2)}) collective-permute-start(f32[65,1,130]{2,1,0:T(1,128)S(1)} %collective-permute-done.5), channel_id=1, source_target_pairs={{0,64},{64,0},{8,72},{72,8},{16,80},{80,16},{24,88},{88,24},{32,96... | collective-permute-start | bytes 101408 | tf_op jit(solution)/shard_map/ppermute | solution.py:30
  43.4 4.8 %collective-permute-done.6 = f32[65,1,130]{2,1,0:T(1,128)S(1)} collective-permute-done((f32[65,1,130]{2,1,0:T(1,128)S(1)}, f32[65,1,130]{2,1,0:T(1,128)S(1)}, u32[]{:S(2)}, u32[]{:S(2)}) %collective-permute-start.6) | collective-permute-done | bytes 33832 | tf_op jit(solution)/shard_map/ppermute | solution.py:30
  48.2 1.1 collective-permute-start.7
  49.3 5.1 %collective-permute-start.8 = (f32[65,1,130]{2,1,0:T(1,128)S(1)}, f32[65,1,130]{2,1,0:T(1,128)S(1)}, u32[]{:S(2)}, u32[]{:S(2)}) collective-permute-start(f32[65,1,130]{2,1,0:T(1,128)S(1)} %get-tuple-element.4), channel_id=1, source_target_pairs={{1,0},{2,1},{3,2},{4,3},{5,4},{6,5},{7,6},{9,8},{10,9},{11,10},{12... | collective-permute-start | bytes 101408 | tf_op jit(solution)/shard_map/ppermute | solution.py:18
  54.4 2.4 %collective-permute-start.2 = (f32[65,1,130]{2,1,0:T(1,128)S(1)}, f32[65,1,130]{2,1,0:T(1,128)S(1)}, u32[]{:S(2)}, u32[]{:S(2)}) collective-permute-start(f32[65,1,130]{2,1,0:T(1,128)S(1)} %get-tuple-element.3), channel_id=1, source_target_pairs={{0,1},{1,2},{2,3},{3,4},{4,5},{5,6},{6,7},{8,9},{9,10},{10,11},{11... | collective-permute-start | bytes 101408 | tf_op jit(solution)/shard_map/ppermute | solution.py:17
  56.9 0.7 reverse
  57.6 0.3 broadcast_select_fusion
  57.9 5.1 %collective-permute-done.2 = f32[65,1,130]{2,1,0:T(1,128)S(1)} collective-permute-done((f32[65,1,130]{2,1,0:T(1,128)S(1)}, f32[65,1,130]{2,1,0:T(1,128)S(1)}, u32[]{:S(2)}, u32[]{:S(2)}) %collective-permute-start.2) | collective-permute-done | bytes 33832 | tf_op jit(solution)/shard_map/ppermute | solution.py:17
  63.0 1.0 fusion.58
  64.1 0.2 fusion
  64.2 1.6 %fusion.57 = f32[15,128,128]{2,1,0:T(8,128)} fusion(f32[16,130,130]{2,1,0:T(8,128)S(1)} %fusion, f32[16,128,128]{2,1,0:T(8,128)S(1)} %copy-done.2, f32[16,128,128]{2,1,0:T(8,128)S(1)} %copy-done.4), kind=kLoop, calls=%fused_computation.87 | loop fusion | flops 1474560 | bytes 6881280 | tf_op jit(solution)/shard_map/mul | solution.py:80
  65.8 16.1 %fusion.40 = f32[16,128,128]{2,1,0:T(8,128)} fusion(f32[16,128,128]{2,1,0:T(8,128)} %param.7, f32[16,128,128]{2,1,0:T(8,128)} %param.10, f32[65,1,130]{2,1,0:T(1,128)S(1)} %broadcast_select_fusion, f32[65,128,1]{2,1,0:T(8,128)} %copy.13, f32[65,128,128]{2,1,0:T(8,128)S(1)} %bitcast.8, f32[65,128,1]{2,1,0:T(8,128)} %copy.12, ...), kind=kLoop, calls=%fused_computation.58 | loop fusion | flops 19922944 | bytes 15862800 | tf_op jit(solution)/shard_map/mul | solution.py:83
  81.9 1.3 fusion.62
  83.2 1.7 %fusion.61 = (f32[16,128,1]{2,1,0:T(8,128)}, f32[16,128,1]{2,1,0:T(8,128)}) fusion(f32[16,128,128]{2,1,0:T(8,128)S(1)} %fusion.62), kind=kLoop, calls=%fused_computation.109 | loop fusion | bytes 32768 | tf_op jit(solution)/shard_map/slice | solution.py:16
  84.9 1.6 %copy.16 = f32[16,128,1]{1,0,2:T(8,128)S(1)} copy(f32[16,128,1]{2,1,0:T(8,128)} %get-tuple-element.9) | data formatting | bytes 16384 | tf_op jit(solution)/shard_map/slice | solution.py:16
  86.5 1.6 %copy.18 = f32[16,128,1]{1,0,2:T(8,128)S(1)} copy(f32[16,128,1]{2,1,0:T(8,128)} %get-tuple-element.10) | data formatting | bytes 16384 | tf_op jit(solution)/shard_map/slice | solution.py:15
  88.1 0.5 collective-permute-start.10
  88.6 1.3 copy.17
  90.0 3.4 %collective-permute-done.10 = f32[16,128,1]{1,0,2:T(8,128)S(1)} collective-permute-done((f32[16,128,1]{1,0,2:T(8,128)S(1)}, f32[16,128,1]{1,0,2:T(8,128)S(1)}, u32[]{:S(2)}, u32[]{:S(2)}) %collective-permute-start.10) | collective-permute-done | bytes 8224 | tf_op jit(solution)/shard_map/ppermute | solution.py:17
  93.3 1.4 copy.19
  94.7 1.1 pad_maximum_fusion.31
  95.9 1.2 collective-permute-done.11
  97.1 3.7 %collective-permute-done.12 = f32[16,1,130]{2,1,0:T(1,128)S(1)} collective-permute-done((f32[16,1,130]{2,1,0:T(1,128)S(1)}, f32[16,1,130]{2,1,0:T(1,128)S(1)}, u32[]{:S(2)}, u32[]{:S(2)}) %collective-permute-start.12) | collective-permute-done | bytes 8352 | tf_op jit(solution)/shard_map/ppermute | solution.py:30
  100.8 0.3 collective-permute-start.13
  101.1 4.3 %collective-permute-done.13 = f32[16,1,130]{2,1,0:T(1,128)S(1)} collective-permute-done((f32[16,1,130]{2,1,0:T(1,128)S(1)}, f32[16,1,130]{2,1,0:T(1,128)S(1)}, u32[]{:S(2)}, u32[]{:S(2)}) %collective-permute-start.13) | collective-permute-done | bytes 8352 | tf_op jit(solution)/shard_map/ppermute | solution.py:30
  105.4 2.9 %collective-permute-start.14 = (f32[16,1,130]{2,1,0:T(1,128)S(1)}, f32[16,1,130]{2,1,0:T(1,128)S(1)}, u32[]{:S(2)}, u32[]{:S(2)}) collective-permute-start(f32[16,1,130]{2,1,0:T(1,128)S(1)} %collective-permute-done.13), channel_id=1, source_target_pairs={{0,64},{64,0},{8,72},{72,8},{16,80},{80,16},{24,88},{88,24},{32,96... | collective-permute-start | bytes 24968 | tf_op jit(solution)/shard_map/ppermute | solution.py:30
  108.4 1.9 %collective-permute-start.17 = (f32[16,1,130]{2,1,0:T(1,128)S(1)}, f32[16,1,130]{2,1,0:T(1,128)}, u32[]{:S(2)}, u32[]{:S(2)}) collective-permute-start(f32[16,1,130]{2,1,0:T(1,128)S(1)} %get-tuple-element.8), channel_id=1, source_target_pairs={{0,1},{1,2},{2,3},{3,4},{4,5},{5,6},{6,7},{8,9},{9,10},{10,11},{11... | collective-permute-start | bytes 24968 | tf_op jit(solution)/shard_map/ppermute | solution.py:17
  110.3 6.3 %collective-permute-start.16 = (f32[16,1,130]{2,1,0:T(1,128)S(1)}, f32[16,1,130]{2,1,0:T(1,128)S(1)}, u32[]{:S(2)}, u32[]{:S(2)}) collective-permute-start(f32[16,1,130]{2,1,0:T(1,128)S(1)} %get-tuple-element.7), channel_id=1, source_target_pairs={{1,0},{2,1},{3,2},{4,3},{5,4},{6,5},{7,6},{9,8},{10,9},{11,10},{12... | collective-permute-start | bytes 24968 | tf_op jit(solution)/shard_map/ppermute | solution.py:18
  116.7 0.4 collective-permute-start.15
  117.1 8.7 %fusion.25 = f32[16,128,128]{2,1,0:T(8,128)} fusion(f32[16,128,128]{2,1,0:T(8,128)} %param.8, f32[65,1,130]{2,1,0:T(1,128)S(1)} %collective-permute-done.2, f32[65,128,1]{2,1,0:T(8,128)} %copy.13, f32[65,128,128]{2,1,0:T(8,128)} %copy-done, f32[65,128,1]{2,1,0:T(8,128)} %copy.12, f32[65,1,130]{2,1,0:T(1,128)S(1)} %broadcast_select_fusion, ...), kind=kLoop, calls=%fused_computation.35 | loop fusion | flops 8126464 | bytes 13913616 | tf_op jit(solution)/shard_map/mul | solution.py:102
  125.8 0.6 copy-done.8
  126.4 1.0 reverse.1
  127.4 0.1 broadcast_select_fusion.1
  127.5 9.4 %fusion.11 = f32[16,128,128]{2,1,0:T(8,128)} fusion(f32[16,128,128]{2,1,0:T(8,128)} %param.9, f32[65,128,128]{2,1,0:T(8,128)} %copy-done, f32[65,128,1]{2,1,0:T(8,128)} %copy.12, f32[65,128,1]{2,1,0:T(8,128)} %copy.13, f32[16,1,130]{2,1,0:T(1,128)} %collective-permute-done.17, f32[16,128,1]{2,1,0:T(8,128)} %copy.17, f32[16,128,128]{2,1,0:T(8,128)S(1)} %fusion.62, ...), kind=kLoop, calls=%fused_computation.13 | loop fusion | flops 9175040 | bytes 13930256 | tf_op jit(solution)/shard_map/mul | solution.py:111
  (42 shorter events, 0.5 us)
Async XLA Ops:
  0.6 2.8 %copy-start.1 = (f32[16,128,128]{2,1,0:T(8,128)S(1)}, f32[16,128,128]{2,1,0:T(8,128)}, u32[]{:S(2)}) copy-start(f32[16,128,128]{2,1,0:T(8,128)} %param.9) | copy-start | bytes 3145732
  0.6 2.9 %copy-start.3 = (f32[16,128,128]{2,1,0:T(8,128)S(1)}, f32[16,128,128]{2,1,0:T(8,128)}, u32[]{:S(2)}) copy-start(f32[16,128,128]{2,1,0:T(8,128)} %param.10) | copy-start | bytes 3145732
  0.7 3.0 %copy-start.7 = (s32[128,128]{1,0:T(8,128)S(1)}, s32[128,128]{1,0:T(8,128)}, u32[]{:S(2)}) copy-start(s32[128,128]{1,0:T(8,128)} %param.13) | copy-start | bytes 196612
  0.7 3.0 %copy-start.6 = (s32[128,128]{1,0:T(8,128)S(1)}, s32[128,128]{1,0:T(8,128)}, u32[]{:S(2)}) copy-start(s32[128,128]{1,0:T(8,128)} %param.12) | copy-start | bytes 196612
  3.7 4.9 %copy-start = (f32[65,128,128]{2,1,0:T(8,128)}, f32[65,128,128]{2,1,0:T(8,128)S(1)}, u32[]{:S(2)}) copy-start(f32[65,128,128]{2,1,0:T(8,128)S(1)} %bitcast_dynamic-update-slice_fusion) | copy-start | bytes 12779524
  11.5 9.4 %collective-permute-start = (f32[65,128,1]{1,2,0:T(1,128)S(1)}, f32[65,128,1]{1,2,0:T(1,128)S(1)}, u32[]{:S(2)}, u32[]{:S(2)}) collective-permute-start(f32[65,128,1]{1,2,0:T(1,128)S(1)} %copy.10), channel_id=1, source_target_pairs={{0,8},{8,16},{16,24},{24,32},{32,40},{40,48},{48,56},{56,64},{64,7... | collective-permute-start | bytes 99848 | tf_op jit(solution)/shard_map/ppermute | solution.py:17
  14.6 9.2 %collective-permute-start.1 = (f32[65,128,1]{1,2,0:T(1,128)S(1)}, f32[65,128,1]{1,2,0:T(1,128)S(1)}, u32[]{:S(2)}, u32[]{:S(2)}) collective-permute-start(f32[65,128,1]{1,2,0:T(1,128)S(1)} %copy.11), channel_id=1, source_target_pairs={{8,0},{16,8},{24,16},{32,24},{40,32},{48,40},{56,48},{64,56},{72,6... | collective-permute-start | bytes 99848 | tf_op jit(solution)/shard_map/ppermute | solution.py:18
  26.6 31.0 %copy-start.9 = (f32[65]{0:T(128)S(1)}, f32[65]{0:T(128)}, u32[]{:S(2)}) copy-start(f32[65]{0:T(128)} %constant.13.clone.1) | copy-start | bytes 784
  26.6 39.2 %slice-start = ((s8[4259840]{0:T(1024)(128)(4,1)}), s8[65536]{0:T(1024)(128)(4,1)S(1)}, s32[]{:S(2)}) async-start(s8[4259840]{0:T(1024)(128)(4,1)} %bitcast.7), calls=%async_computation | async-start | bytes 131072
  28.5 1.3 collective-permute-start.3
  29.8 4.3 %collective-permute-start.4 = (f32[65,1,130]{2,1,0:T(1,128)S(1)}, f32[65,1,130]{2,1,0:T(1,128)S(1)}, u32[]{:S(2)}, u32[]{:S(2)}) collective-permute-start(f32[65,1,130]{2,1,0:T(1,128)S(1)} %collective-permute-done.3), channel_id=1, source_target_pairs={{0,16},{16,0},{8,24},{24,8},{32,48},{48,32},{40,56},{56,40},{64,80... | collective-permute-start | bytes 101408 | tf_op jit(solution)/shard_map/ppermute | solution.py:30
  34.1 5.9 %collective-permute-start.5 = (f32[65,1,130]{2,1,0:T(1,128)S(1)}, f32[65,1,130]{2,1,0:T(1,128)S(1)}, u32[]{:S(2)}, u32[]{:S(2)}) collective-permute-start(f32[65,1,130]{2,1,0:T(1,128)S(1)} %collective-permute-done.4), channel_id=1, source_target_pairs={{0,32},{32,0},{8,40},{40,8},{16,48},{48,16},{24,56},{56,24},{64,96... | collective-permute-start | bytes 101408 | tf_op jit(solution)/shard_map/ppermute | solution.py:30
  40.0 8.2 %collective-permute-start.6 = (f32[65,1,130]{2,1,0:T(1,128)S(1)}, f32[65,1,130]{2,1,0:T(1,128)S(1)}, u32[]{:S(2)}, u32[]{:S(2)}) collective-permute-start(f32[65,1,130]{2,1,0:T(1,128)S(1)} %collective-permute-done.5), channel_id=1, source_target_pairs={{0,64},{64,0},{8,72},{72,8},{16,80},{80,16},{24,88},{88,24},{32,96... | collective-permute-start | bytes 101408 | tf_op jit(solution)/shard_map/ppermute | solution.py:30
  48.2 8.7 %collective-permute-start.7 = (f32[65,1,130]{2,1,0:T(1,128)S(1)}, f32[65,1,130]{2,1,0:T(1,128)S(1)}, u32[]{:S(2)}, u32[]{:S(2)}) collective-permute-start(f32[65,1,130]{2,1,0:T(1,128)S(1)} %collective-permute-done.6), channel_id=1, source_target_pairs={{0,128},{128,0},{8,136},{136,8},{16,144},{144,16},{24,152},{152,24... | collective-permute-start | bytes 101408 | tf_op jit(solution)/shard_map/ppermute | solution.py:30
  49.3 8.2 %collective-permute-start.8 = (f32[65,1,130]{2,1,0:T(1,128)S(1)}, f32[65,1,130]{2,1,0:T(1,128)S(1)}, u32[]{:S(2)}, u32[]{:S(2)}) collective-permute-start(f32[65,1,130]{2,1,0:T(1,128)S(1)} %get-tuple-element.4), channel_id=1, source_target_pairs={{1,0},{2,1},{3,2},{4,3},{5,4},{6,5},{7,6},{9,8},{10,9},{11,10},{12... | collective-permute-start | bytes 101408 | tf_op jit(solution)/shard_map/ppermute | solution.py:18
  54.4 8.6 %collective-permute-start.2 = (f32[65,1,130]{2,1,0:T(1,128)S(1)}, f32[65,1,130]{2,1,0:T(1,128)S(1)}, u32[]{:S(2)}, u32[]{:S(2)}) collective-permute-start(f32[65,1,130]{2,1,0:T(1,128)S(1)} %get-tuple-element.3), channel_id=1, source_target_pairs={{0,1},{1,2},{2,3},{3,4},{4,5},{5,6},{6,7},{8,9},{9,10},{10,11},{11... | collective-permute-start | bytes 101408 | tf_op jit(solution)/shard_map/ppermute | solution.py:17
  57.8 6.4 %copy-start.2 = (f32[16,128,128]{2,1,0:T(8,128)S(1)}, f32[16,128,128]{2,1,0:T(8,128)}, u32[]{:S(2)}) copy-start(f32[16,128,128]{2,1,0:T(8,128)} %param.7) | copy-start | bytes 3145732
  57.9 6.4 %copy-start.4 = (f32[16,128,128]{2,1,0:T(8,128)S(1)}, f32[16,128,128]{2,1,0:T(8,128)}, u32[]{:S(2)}) copy-start(f32[16,128,128]{2,1,0:T(8,128)} %param.10) | copy-start | bytes 3145732
  57.9 7.9 %slice-start.1 = ((s8[4259840]{0:T(1024)(128)(4,1)}), s8[4194304]{0:T(1024)(128)(4,1)S(1)}, s32[]{:S(2)}) async-start(s8[4259840]{0:T(1024)(128)(4,1)} %bitcast.7), calls=%async_computation.1 | async-start | bytes 8388608
  84.9 32.2 %copy-start.5 = (f32[128,128]{1,0:T(8,128)S(1)}, f32[128,128]{1,0:T(8,128)}, u32[]{:S(2)}) copy-start(f32[128,128]{1,0:T(8,128)} %param.11) | copy-start | bytes 196612
  86.5 2.2 %collective-permute-start.9 = (f32[16,128,1]{1,0,2:T(8,128)S(1)}, f32[16,128,1]{1,0,2:T(8,128)S(1)}, u32[]{:S(2)}, u32[]{:S(2)}) collective-permute-start(f32[16,128,1]{1,0,2:T(8,128)S(1)} %copy.16), channel_id=1, source_target_pairs={{8,0},{16,8},{24,16},{32,24},{40,32},{48,40},{56,48},{64,56},{72,6... | collective-permute-start | bytes 24584 | tf_op jit(solution)/shard_map/ppermute | solution.py:18
  88.1 5.2 %collective-permute-start.10 = (f32[16,128,1]{1,0,2:T(8,128)S(1)}, f32[16,128,1]{1,0,2:T(8,128)S(1)}, u32[]{:S(2)}, u32[]{:S(2)}) collective-permute-start(f32[16,128,1]{1,0,2:T(8,128)S(1)} %copy.18), channel_id=1, source_target_pairs={{0,8},{8,16},{16,24},{24,32},{32,40},{40,48},{48,56},{56,64},{64,7... | collective-permute-start | bytes 24584 | tf_op jit(solution)/shard_map/ppermute | solution.py:17
  95.8 1.3 collective-permute-start.11
  97.1 3.7 %collective-permute-start.12 = (f32[16,1,130]{2,1,0:T(1,128)S(1)}, f32[16,1,130]{2,1,0:T(1,128)S(1)}, u32[]{:S(2)}, u32[]{:S(2)}) collective-permute-start(f32[16,1,130]{2,1,0:T(1,128)S(1)} %collective-permute-done.11), channel_id=1, source_target_pairs={{0,16},{16,0},{8,24},{24,8},{32,48},{48,32},{40,56},{56,40},{64,80... | collective-permute-start | bytes 24968 | tf_op jit(solution)/shard_map/ppermute | solution.py:30
  100.8 4.6 %collective-permute-start.13 = (f32[16,1,130]{2,1,0:T(1,128)S(1)}, f32[16,1,130]{2,1,0:T(1,128)S(1)}, u32[]{:S(2)}, u32[]{:S(2)}) collective-permute-start(f32[16,1,130]{2,1,0:T(1,128)S(1)} %collective-permute-done.12), channel_id=1, source_target_pairs={{0,32},{32,0},{8,40},{40,8},{16,48},{48,16},{24,56},{56,24},{64,96... | collective-permute-start | bytes 24968 | tf_op jit(solution)/shard_map/ppermute | solution.py:30
  105.4 11.2 %collective-permute-start.14 = (f32[16,1,130]{2,1,0:T(1,128)S(1)}, f32[16,1,130]{2,1,0:T(1,128)S(1)}, u32[]{:S(2)}, u32[]{:S(2)}) collective-permute-start(f32[16,1,130]{2,1,0:T(1,128)S(1)} %collective-permute-done.13), channel_id=1, source_target_pairs={{0,64},{64,0},{8,72},{72,8},{16,80},{80,16},{24,88},{88,24},{32,96... | collective-permute-start | bytes 24968 | tf_op jit(solution)/shard_map/ppermute | solution.py:30
  108.4 19.1 %collective-permute-start.17 = (f32[16,1,130]{2,1,0:T(1,128)S(1)}, f32[16,1,130]{2,1,0:T(1,128)}, u32[]{:S(2)}, u32[]{:S(2)}) collective-permute-start(f32[16,1,130]{2,1,0:T(1,128)S(1)} %get-tuple-element.8), channel_id=1, source_target_pairs={{0,1},{1,2},{2,3},{3,4},{4,5},{5,6},{6,7},{8,9},{9,10},{10,11},{11... | collective-permute-start | bytes 24968 | tf_op jit(solution)/shard_map/ppermute | solution.py:17
  110.3 17.1 %collective-permute-start.16 = (f32[16,1,130]{2,1,0:T(1,128)S(1)}, f32[16,1,130]{2,1,0:T(1,128)S(1)}, u32[]{:S(2)}, u32[]{:S(2)}) collective-permute-start(f32[16,1,130]{2,1,0:T(1,128)S(1)} %get-tuple-element.7), channel_id=1, source_target_pairs={{1,0},{2,1},{3,2},{4,3},{5,4},{6,5},{7,6},{9,8},{10,9},{11,10},{12... | collective-permute-start | bytes 24968 | tf_op jit(solution)/shard_map/ppermute | solution.py:18
  116.7 9.1 %collective-permute-start.15 = (f32[16,1,130]{2,1,0:T(1,128)S(1)}, f32[16,1,130]{2,1,0:T(1,128)S(1)}, u32[]{:S(2)}, u32[]{:S(2)}) collective-permute-start(f32[16,1,130]{2,1,0:T(1,128)S(1)} %collective-permute-done.14), channel_id=1, source_target_pairs={{0,128},{128,0},{8,136},{136,8},{16,144},{144,16},{24,152},{152,24... | collective-permute-start | bytes 24968 | tf_op jit(solution)/shard_map/ppermute | solution.py:30
  125.8 0.6 copy-start.8
where the time goes:
time: 138 us; the launch traced here: 137 us
  other arithmetic  41.7 us (30%)
  starting transfers between devices  33.1 us (24%)
  waiting for transfers between devices  32.1 us (23%)
  local copies, waits for them, and re-layouts  29.1 us (21%)
    ppermute x10, waiting for transfers between devices, partner(): return lax.ppermute(block, axis, route)  23.6 us
    ppermute x4, starting transfers between devices, extended_2(): after = lax.ppermute(first, axis, down)  17.9 us
    mul x1, other arithmetic, tracer_step(): w_mid * (t_mid + DT * (flux_west - flux_east + flux_south - flux_north +...  16.1 us
    ppermute x10, starting transfers between devices, partner(): return lax.ppermute(block, axis, route)  10.3 us
    mul x1, other arithmetic, momentum_step(): w_mid * (v_mid + DT * (-coriolis * u_mid - GRAV * 0.5 * (p_north - p_sout...  9.43 us
    slice x3, local copies, waits for them, and re-layouts, extended_2(): last = lax.slice_in_dim(x, length - width, length, axis=dim)  9.39 us
    mul x1, other arithmetic, momentum_step(): w_mid * (u_mid + DT * (coriolis * v_mid - GRAV * 0.5 * (p_east - p_west)...  8.66 us
    ppermute x4, waiting for transfers between devices, extended_2(): before = lax.ppermute(last, axis, up)  8.51 us
  transfers between devices with their start and end apart: 18, of which 9 were waited for; matrix products, arithmetic and copies ran while one was open for 14% of the time, Pallas kernels for 0%

commit v1 on v0

v1 whole, which is shorter than its diff:
```python
import functools
import math

import jax
import jax.numpy as jnp
from jax import lax
from jax.experimental import pallas as pl
from jax.experimental.pallas import tpu as pltpu
from jax.sharding import PartitionSpec as P

MESH = pl.DeviceIdType.MESH
NK = 16
N = 128
FLAT = NK * N
PAD = N + 8
SCALE = 1.0 / 16.0
PG = 0.25 * 0.05
WEST, EAST, SOUTH, NORTH = 0, 1, 2, 3
MSG = 4 * NK + 8


def east_of(x):
    return pltpu.roll(x, N - 1, 1)


def west_of(x):
    return pltpu.roll(x, 1, 1)


def face(c, d, a, b, ta, tb, ka, kb):
    return jnp.where(c < d, (a + b) * (ta + tb) - (ka + kb) * (tb - ta), 0.0)


def mirrored(x):
    lane = lax.broadcasted_iota(jnp.int32, x.shape, 1)
    for bit in (1, 2, 4, 8, 16, 32, 64):
        x = jnp.where((lane & bit) == 0, pltpu.roll(x, N - bit, 1), pltpu.roll(x, bit, 1))
    return x


def running_sum(x):
    level = lax.broadcasted_iota(jnp.int32, x.shape, 0)
    for step in (1, 2, 4, 8):
        x = x + jnp.where(level >= step, pltpu.roll(x, step, 0), 0.0)
    return x


def kernel(
    n_lon, n_lat,
    t_hbm, u_hbm, v_hbm, k_hbm, fr_hbm, ind_hbm, str_hbm,
    tn, un, vn,
    t, u, v, kd, p, fa, fb, fr, ind, strata, dep, dep_e, dep_n, cor,
    tiles, fix, send, recv, psend, precv,
    in_sem, send_sem, recv_sem, psend_sem, precv_sem,
):
    lon, lat = lax.axis_index("lon"), lax.axis_index("lat")
    is_top, is_bottom = lat == n_lat - 1, lat == 0
    east = (lat, lax.rem(lon + 1, n_lon))
    west = (lat, lax.rem(lon + n_lon - 1, n_lon))
    north = (jnp.where(is_top, lat, lat + 1), jnp.where(is_top, n_lon - 1 - lon, lon))
    south = (jnp.where(is_bottom, lat, lat - 1), lon)

    def at(place):
        return {"lat": place[0], "lon": place[1]}

    loads = [
        pltpu.make_async_copy(src, dst, in_sem.at[i])
        for i, (src, dst) in enumerate(
            (
                (ind_hbm, ind), (str_hbm, strata), (fr_hbm, fr),
                (t_hbm, t.at[pl.ds(0, FLAT)]), (u_hbm, u.at[pl.ds(0, FLAT)]),
                (k_hbm, kd.at[pl.ds(0, FLAT)]), (v_hbm, v.at[pl.ds(0, FLAT)]),
            )
        )
    ]
    for load in loads:
        load.start()
    barrier = pltpu.get_barrier_semaphore()
    for place in (west, east, north):
        pl.semaphore_signal(barrier, inc=1, device_id=at(place), device_id_type=MESH)

    @pl.when(jnp.logical_not(is_bottom))
    def _():
        pl.semaphore_signal(barrier, inc=1, device_id=at(south), device_id_type=MESH)

    lane8 = lax.broadcasted_iota(jnp.int32, (8, N), 1)
    group = lane8 >> 2
    zero8 = jnp.zeros((8, N), jnp.float32)
    lane = lax.broadcasted_iota(jnp.int32, (NK, N), 1)
    level = lax.broadcasted_iota(jnp.int32, (NK, N), 0).astype(jnp.float32)
    first, last = lane == 0, lane == N - 1

    for k in range(NK + 1):
        p[pl.ds(k * PAD, 8), :] = zero8
        fa[pl.ds(k * PAD, 8), :] = zero8
        fb[pl.ds(k * PAD, 8), :] = zero8

    @pl.when(is_bottom)
    def _():
        recv[SOUTH] = jnp.zeros((MSG, N), jnp.float32)
        precv[SOUTH] = jnp.zeros((NK, N), jnp.float32)

    def set_cor(b, _):
        rows = pl.ds(pl.multiple_of(b * 8, 8), 8)
        j = lax.broadcasted_iota(jnp.int32, (8, N), 0) + (b * 8 + lat * N)
        cor[rows, :] = 0.25 * jnp.sin(
            jnp.pi * ((j.astype(jnp.float32) + 0.5) / (N * n_lat) - 0.5)
        )
        return 0

    lax.fori_loop(0, N // 8, set_cor, 0)

    for load in loads[:3]:
        load.wait()
    dep[pl.ds(N, 8), :] = zero8
    dep[pl.ds(0, N), :] = (ind[...] * strata[...]).astype(jnp.float32)
    fr[...] = fr[...] * 0.25

    def set_depth(b, _):
        r = pl.multiple_of(b * 8, 8)
        rows = pl.ds(r, 8)
        d = dep[rows, :]
        dep_e[rows, :] = jnp.where(lane8 == N - 1, 0.0, jnp.minimum(d, east_of(d)))
        dep_n[rows, :] = jnp.minimum(d, dep[pl.ds(r + 1, 8), :])
        x = pltpu.roll(d, 2, 1)
        y = pltpu.roll(fr[rows, :], 6, 1)
        tiles[2, rows, :] = jnp.where(group == 0, x, jnp.where(group == 1, y, 0.0))
        return 0

    lax.fori_loop(0, N // 8, set_depth, 0)

    def pack(f, tile, a, b, double):
        def step(i, _):
            r = pl.multiple_of(i * 8, 8)
            parts = []
            for q in range(2 * NK):
                ref = a if q < NK else b
                rows = pl.ds(r + (q % NK) * N, 8)
                x = ref[rows, :]
                if double and q < NK:
                    x = x + x
                    ref[rows, :] = x
                y = pltpu.roll(x, (2 + 4 * q) % N, 1)
                parts.append(y if q % 4 == 0 else jnp.where(group == q, y, parts.pop()))
            acc = parts[0]
            for g in range(1, 8):
                acc = jnp.where(group >= 4 * g, parts[g], acc)
            tiles[tile, pl.ds(r, 8), :] = acc
            return 0

        lax.fori_loop(0, N // 8, step, 0)
        tiles[tile] = tiles[tile].T

    tiles[2] = tiles[2].T
    loads[3].wait()
    loads[4].wait()
    pack(0, 0, t, u, False)
    loads[5].wait()
    loads[6].wait()
    pack(1, 1, kd, v, True)

    def column(tile, half, entry):
        return tiles[tile, pl.ds(64 * half + entry, NK, stride=4), :]

    def columns(entry):
        return (
            column(0, 0, entry), column(0, 1, entry), column(1, 1, entry), column(1, 0, entry),
            jnp.broadcast_to(tiles[2, pl.ds(entry, 1), :], (NK, N)),
        )

    def row(ref, j):
        return ref[pl.ds(j, NK, stride=N), :]

    def edge_rows(j):
        return (
            row(t, j), row(u, j), row(v, j), row(kd, j),
            jnp.broadcast_to(dep[pl.ds(j, 1), :], (NK, N)),
        )

    def stage(side, values):
        for f in range(4):
            send[side, pl.ds(f * NK, NK), :] = values[f]
        send[side, pl.ds(4 * NK, 8), :] = values[4][:8]

    stage(EAST, columns(1))
    stage(WEST, columns(2))
    stage(NORTH, edge_rows(N - 1))
    stage(SOUTH, edge_rows(0))

    pl.semaphore_wait(barrier, jnp.where(is_bottom, 3, 4))
    north_slot = jnp.where(is_top, NORTH, SOUTH)

    def exchange(out, into, out_sem, into_sem):
        def copy(side, slot, place):
            return pltpu.make_async_remote_copy(
                src_ref=out.at[side], dst_ref=into.at[slot], send_sem=out_sem.at[side],
                recv_sem=into_sem.at[slot], device_id=at(place), device_id_type=MESH,
            )

        sends = [
            copy(EAST, WEST, east), copy(WEST, EAST, west), copy(NORTH, north_slot, north),
        ]
        down = copy(SOUTH, NORTH, south)

        def start():
            for s in sends:
                s.start()

            @pl.when(jnp.logical_not(is_bottom))
            def _():
                down.start()

        def wait_recv():
            copy(WEST, WEST, west).wait_recv()
            copy(EAST, EAST, east).wait_recv()
            copy(NORTH, NORTH, north).wait_recv()

            @pl.when(jnp.logical_not(is_bottom))
            def _():
                copy(SOUTH, SOUTH, south).wait_recv()

        def wait_send():
            for s in sends:
                s.wait_send()

            @pl.when(jnp.logical_not(is_bottom))
            def _():
                down.wait_send()

        return start, wait_recv, wait_send

    start1, arrive1, sent1 = exchange(send, recv, send_sem, recv_sem)
    start2, arrive2, sent2 = exchange(psend, precv, psend_sem, precv_sem)
    start1()

    def tracer(b, _):
        r = pl.multiple_of(b * 8, 8)
        rows = pl.ds(r, 8)
        d, de, dn = dep[rows, :], dep_e[rows, :], dep_n[rows, :]
        below = zero8
        for k in range(NK):
            c = float(k)
            here, up_rows = pl.ds(r + k * N, 8), pl.ds(r + k * N + 1, 8)
            tc, kc, uc, vc = t[here, :], kd[here, :], u[here, :], v[here, :]
            f_e = face(c, de, uc, east_of(uc), tc, east_of(tc), kc, east_of(kc))
            f_n = face(c, dn, vc, v[up_rows, :], tc, t[up_rows, :], kc, kd[up_rows, :])
            fa[pl.ds(r + k * PAD + 8, 8), :] = f_n
            f_s = fa[pl.ds(r + k * PAD + 7, 8), :]
            if k < NK - 1:
                t_up, k_up = t[pl.ds(r + (k + 1) * N, 8), :], kd[pl.ds(r + (k + 1) * N, 8), :]
                above = jnp.where(c + 1.0 < d, (kc + k_up) * (t_up - tc), 0.0)
            else:
                above = zero8
            total = (west_of(f_e) - f_e) + (f_s - f_n) + (above - below)
            below = above
            tn[here, :] = jnp.where(c < d, tc + SCALE * total, 0.0)
        return 0

    lax.fori_loop(0, N // 8, tracer, 0)

    arrive1()

    @pl.when(is_top)
    def _():
        x = mirrored(recv[NORTH])
        sign = lax.broadcasted_iota(jnp.int32, (MSG, N), 0)
        recv[NORTH] = jnp.where((sign >= NK) & (sign < 3 * NK), -x, x)

    def ghost(slot):
        parts = [recv[slot, pl.ds(f * NK, NK), :] for f in range(4)]
        d = recv[slot, pl.ds(4 * NK, 1), :]
        return (*parts, jnp.broadcast_to(d, (NK, N)))

    g_w, g_e, g_s, g_n = ghost(WEST), ghost(EAST), ghost(SOUTH), ghost(NORTH)

    def x_face(a, b):
        return face(level, jnp.minimum(a[4], b[4]), a[1], b[1], a[0], b[0], a[3], b[3])

    def y_face(a, b):
        return face(level, jnp.minimum(a[4], b[4]), a[2], b[2], a[0], b[0], a[3], b[3])

    def column_step(mid, left, right, north_corner, south_corner):
        up = tuple(jnp.where(last, c, east_of(m)) for m, c in zip(mid, north_corner))
        down = tuple(jnp.where(first, c, west_of(m)) for m, c in zip(mid, south_corner))
        tc, _, _, kc, d = mid
        above = jnp.where(
            level + 1.0 < d,
            (kc + pltpu.roll(kc, NK - 1, 0)) * (pltpu.roll(tc, NK - 1, 0) - tc),
            0.0,
        )
        below = pltpu.roll(above, 1, 0)
        total = (
            (x_face(left, mid) - x_face(mid, right))
            + (y_face(down, mid) - y_face(mid, up))
            + (above - below)
        )
        return jnp.where(level < d, tc + SCALE * total, 0.0)

    c_e, c_w = columns(1), columns(2)
    t_w = column_step(
        c_w, g_w, columns(3), tuple(east_of(x) for x in g_n), g_s
    )
    t_e = column_step(
        c_e, columns(0), g_e, g_n, tuple(west_of(x) for x in g_s)
    )
    r_s, r_n = edge_rows(0), edge_rows(N - 1)
    t_n = row(tn, N - 1) - SCALE * y_face(r_n, g_n)
    t_s = row(tn, 0) + SCALE * y_face(g_s, r_s)
    t_n = jnp.where(first, west_of(t_w), jnp.where(last, t_e, t_n))
    t_s = jnp.where(first, t_w, jnp.where(last, east_of(t_e), t_s))
    p_w, p_e = running_sum(PG * t_w), running_sum(PG * t_e)
    psend[EAST] = p_e
    psend[WEST] = p_w
    psend[NORTH] = running_sum(PG * t_n)
    psend[SOUTH] = running_sum(PG * t_s)
    start2()

    tn[pl.ds(N - 1, NK, stride=N), :] = t_n
    tn[pl.ds(0, NK, stride=N), :] = t_s
    fix[pl.ds(0, NK, stride=2), :] = t_e
    fix[pl.ds(1, NK, stride=2), :] = t_w
    for q in range(4, 16):
        fix[pl.ds(q * 8, 8), :] = zero8
    fix[...] = fix[...].T
    rim8 = (lane8 == 0) | (lane8 == N - 1)

    def pressure(b, _):
        r = pl.multiple_of(b * 8, 8)
        x = fix[pl.ds(r, 8), :]
        total = zero8
        for k in range(NK):
            here = pl.ds(r + k * N, 8)
            tc = jnp.where(rim8, pltpu.roll(x, N - 1 - 2 * k, 1), tn[here, :])
            tn[here, :] = tc
            total = total + PG * tc
            p[pl.ds(r + k * PAD + 8, 8), :] = total
        return 0

    lax.fori_loop(0, N // 8, pressure, 0)

    def momentum(b, _):
        r = pl.multiple_of(b * 8, 8)
        rows = pl.ds(r, 8)
        d, de, dn = dep[rows, :], dep_e[rows, :], dep_n[rows, :]
        f, co = fr[rows, :], cor[rows, :]
        for k in range(NK):
            c = float(k)
            here, up_rows = pl.ds(r + k * N, 8), pl.ds(r + k * N + 1, 8)
            mine, south_rows = pl.ds(r + k * PAD + 8, 8), pl.ds(r + k * PAD + 7, 8)
            uc, vc, pc = u[here, :], v[here, :], p[mine, :]
            wet_e, wet_n, wet = c < de, c < dn, c < d
            u_e = jnp.where(wet_e, east_of(uc) - uc, 0.0)
            v_e = jnp.where(wet_e, east_of(vc) - vc, 0.0)
            u_n = jnp.where(wet_n, u[up_rows, :] - uc, 0.0)
            v_n = jnp.where(wet_n, v[up_rows, :] - vc, 0.0)
            fa[mine, :] = u_n
            fb[mine, :] = v_n
            lap_u = (u_e - west_of(u_e)) + (u_n - fa[south_rows, :])
            lap_v = (v_e - west_of(v_e)) + (v_n - fb[south_rows, :])
            dp_x = east_of(pc) - west_of(pc)
            dp_y = p[pl.ds(r + k * PAD + 9, 8), :] - p[south_rows, :]
            un[here, :] = jnp.where(wet, (uc + co * vc) - dp_x + f * lap_u, 0.0)
            vn[here, :] = jnp.where(wet, (vc - co * uc) - dp_y + f * lap_v, 0.0)
        return 0

    lax.fori_loop(0, N // 8, momentum, 0)

    arrive2()

    @pl.when(is_top)
    def _():
        precv[NORTH] = mirrored(precv[NORTH])

    def friction(mid, other, f, i):
        m = level < jnp.minimum(mid[4], other[4])
        return jnp.where(m, f * (other[i] - mid[i]), 0.0)

    def masked(mid, x):
        return jnp.where(level < mid[4], x, 0.0)

    f_e = jnp.broadcast_to(tiles[2, pl.ds(5, 1), :], (NK, N))
    f_w = jnp.broadcast_to(tiles[2, pl.ds(6, 1), :], (NK, N))
    f_s = jnp.broadcast_to(fr[pl.ds(0, 1), :], (NK, N))
    f_n = jnp.broadcast_to(fr[pl.ds(N - 1, 1), :], (NK, N))
    up, down = pl.ds(N - 1, NK, stride=N), pl.ds(0, NK, stride=N)
    un[up, :] = un[up, :] + friction(r_n, g_n, f_n, 1)
    un[down, :] = un[down, :] + friction(r_s, g_s, f_s, 1)
    vn[up, :] = vn[up, :] + friction(r_n, g_n, f_n, 2) - masked(r_n, precv[NORTH])
    vn[down, :] = vn[down, :] + friction(r_s, g_s, f_s, 2) + masked(r_s, precv[SOUTH])
    fix[pl.ds(0, NK, stride=2), :] = friction(c_e, g_e, f_e, 1) - masked(c_e, precv[EAST] - p_w)
    fix[pl.ds(1, NK, stride=2), :] = friction(c_w, g_w, f_w, 1) + masked(c_w, precv[WEST] - p_e)
    fix[pl.ds(32, NK, stride=2), :] = friction(c_e, g_e, f_e, 2)
    fix[pl.ds(33, NK, stride=2), :] = friction(c_w, g_w, f_w, 2)
    fix[...] = fix[...].T

    def finish(b, _):
        r = pl.multiple_of(b * 8, 8)
        x = fix[pl.ds(r, 8), :]
        for k in range(NK):
            here = pl.ds(r + k * N, 8)
            un[here, :] = un[here, :] + jnp.where(rim8, pltpu.roll(x, N - 1 - 2 * k, 1), 0.0)
            vn[here, :] = vn[here, :] + jnp.where(rim8, pltpu.roll(x, N - 33 - 2 * k, 1), 0.0)
        return 0

    lax.fori_loop(0, N // 8, finish, 0)
    sent1()
    sent2()


def solution(mesh):
    n_lon, n_lat = mesh.shape["lon"], mesh.shape["lat"]
    f32, i32 = jnp.float32, jnp.int32

    def on_device(t, u, v, kd, fr, ind, strata):
        flat = [x.reshape(FLAT, N) for x in (t, u, v, kd)]
        outs = pl.pallas_call(
            functools.partial(kernel, n_lon, n_lat),
            out_shape=[pltpu.VMEM((FLAT, N), f32)] * 3,
            in_specs=[pl.BlockSpec(memory_space=pltpu.HBM)] * 7,
            out_specs=[pl.BlockSpec(memory_space=pltpu.VMEM)] * 3,
            scratch_shapes=[
                *[pltpu.VMEM((FLAT + 8, N), f32)] * 4,
                *[pltpu.VMEM((NK * PAD + 8, N), f32)] * 3,
                pltpu.VMEM((N, N), f32),
                pltpu.VMEM((N, N), i32),
                pltpu.VMEM((N, N), i32),
                pltpu.VMEM((N + 8, N), f32),
                *[pltpu.VMEM((N, N), f32)] * 3,
                pltpu.VMEM((3, N, N), f32),
                pltpu.VMEM((N, N), f32),
                pltpu.VMEM((4, MSG, N), f32),
                pltpu.VMEM((4, MSG, N), f32),
                pltpu.VMEM((4, NK, N), f32),
                pltpu.VMEM((4, NK, N), f32),
                pltpu.SemaphoreType.DMA((7,)),
                *[pltpu.SemaphoreType.DMA((4,))] * 4,
            ],
            compiler_params=pltpu.CompilerParams(
                collective_id=0, has_side_effects=True, vmem_limit_bytes=60 * 1024 * 1024
            ),
            cost_estimate=pl.CostEstimate(
                flops=80 * FLAT * N, bytes_accessed=30 * FLAT * N, transcendentals=0
            ),
        )(*flat, fr, ind, strata)
        return tuple(x.reshape(NK, N, N) for x in outs)

    plane, field = P("lat", "lon"), P(None, "lat", "lon")
    return jax.shard_map(
        on_device,
        mesh=mesh,
        in_specs=(field, field, field, field, plane, plane, plane),
        out_specs=(field, field, field),
        check_vma=False,
    )
```

time: 138 us -> 26.9 us (0.19)
  the two profiles are of different devices: /device:TPU:6 before, /device:TPU:23 now
where the time goes in v1:
time: 26.9 us
  Pallas kernels  23.3 us (87%)
  local copies, waits for them, and re-layouts  2.91 us (11%)
  between operations  0.64 us (2%)
    pallas_call x1, Pallas kernels, on_device(): pl.pallas_call(functools.partial(kernel, n_lon, n_lat), out_shape=[pltpu....  23.3 us
    unnamed x3, local copies, waits for them, and re-layouts  2.91 us

profile of v1, /device:TPU:23, one launch (start us, length us, event | category | flops | bytes accessed | tf_op | source)
XLA Modules:
  0.0 26.9 jit_solution(9517252517566401314)
XLA Ops:
  0.6 23.3 %shard_map.94 = (f32[2048,128]{1,0:T(8,128)S(1)}, f32[2048,128]{1,0:T(8,128)S(1)}, f32[2048,128]{1,0:T(8,128)S(1)}) custom-call(f32[2048,128]{1,0:T(8,128)} %bitcast.10, f32[2048,128]{1,0:T(8,128)} %bitcast.11, f32[2048,128]{1,0:T(8,128)} %bitcast.12, f32[2048,128]{1,0:T(8,128)} %bitcast.13, f32[128,128]{1,0:T(8,128)} %fr_hbm.1, s32[128,128]{1,0:T(8,128)} %ind_hbm.1, ...), custom_call_target="tpu_custom_call" | custom-call | flops 20971520 | bytes 7864320 | tf_op jit(solution)/shard_map/pallas_call | solution.py:416
  24.0 1.0 %copy.13 = f32[16,128,128]{2,1,0:T(8,128)} copy(f32[16,128,128]{2,1,0:T(8,128)S(1)} %bitcast.9) | data formatting | bytes 2097152
  24.9 1.0 %copy.14 = f32[16,128,128]{2,1,0:T(8,128)} copy(f32[16,128,128]{2,1,0:T(8,128)S(1)} %bitcast.8) | data formatting | bytes 2097152
  25.9 1.0 %copy.15 = f32[16,128,128]{2,1,0:T(8,128)} copy(f32[16,128,128]{2,1,0:T(8,128)S(1)} %bitcast.7) | data formatting | bytes 2097152

commit v2 on v1

v2 whole, which is shorter than its diff:
```python
import functools
import math

import jax
import jax.numpy as jnp
from jax import lax
from jax.experimental import pallas as pl
from jax.experimental.pallas import tpu as pltpu
from jax.sharding import PartitionSpec as P

MESH = pl.DeviceIdType.MESH
NK = 16
N = 128
FLAT = NK * N
PAD = N + 8
SCALE = 1.0 / 16.0
PG = 0.25 * 0.05
WEST, EAST, SOUTH, NORTH = 0, 1, 2, 3
SW, SE, NW, NE = 0, 1, 2, 3
MSG = 5 * NK + 8


def east_of(x):
    return pltpu.roll(x, N - 1, 1)


def west_of(x):
    return pltpu.roll(x, 1, 1)


def face(c, d, a, b, ta, tb, ka, kb):
    return jnp.where(c < d, (a + b) * (ta + tb) - (ka + kb) * (tb - ta), 0.0)


def mirrored(x):
    lane = lax.broadcasted_iota(jnp.int32, x.shape, 1)
    for bit in (1, 2, 4, 8, 16, 32, 64):
        x = jnp.where((lane & bit) == 0, pltpu.roll(x, N - bit, 1), pltpu.roll(x, bit, 1))
    return x


def running_sum(x):
    level = lax.broadcasted_iota(jnp.int32, x.shape, 0)
    for step in (1, 2, 4, 8):
        x = x + jnp.where(level >= step, pltpu.roll(x, step, 0), 0.0)
    return x


def kernel(
    n_lon, n_lat,
    t_hbm, u_hbm, v_hbm, k_hbm, fr_hbm, ind_hbm, str_hbm,
    tn, un, vn,
    t, u, v, kd, p, fa, fb, fr, ind, strata, dep, dep_e, dep_n, cor,
    cols, fix, send, recv, csend, crecv,
    in_sem, send_sem, recv_sem, csend_sem, crecv_sem,
):
    lon, lat = lax.axis_index("lon"), lax.axis_index("lat")
    is_top, is_bottom = lat == n_lat - 1, lat == 0
    not_bottom = jnp.logical_not(is_bottom)
    lon_e, lon_w = lax.rem(lon + 1, n_lon), lax.rem(lon + n_lon - 1, n_lon)
    lat_n, lat_s = jnp.where(is_top, lat, lat + 1), jnp.where(is_bottom, lat, lat - 1)
    east, west = (lat, lon_e), (lat, lon_w)
    north, south = (lat_n, jnp.where(is_top, n_lon - 1 - lon, lon)), (lat_s, lon)
    fold_e, fold_w = lax.rem(2 * n_lon - 2 - lon, n_lon), lax.rem(n_lon - lon, n_lon)
    own_e = is_top & (fold_e == lon)
    own_w = is_top & (fold_w == lon)
    not_own_e, not_own_w = jnp.logical_not(own_e), jnp.logical_not(own_w)
    north_e = (lat_n, jnp.where(is_top, fold_e, lon_e))
    north_w = (lat_n, jnp.where(is_top, fold_w, lon_w))
    south_e, south_w = (lat_s, lon_e), (lat_s, lon_w)

    def at(place):
        return {"lat": place[0], "lon": place[1]}

    loads = [
        pltpu.make_async_copy(src, dst, in_sem.at[i])
        for i, (src, dst) in enumerate(
            (
                (ind_hbm, ind), (str_hbm, strata), (fr_hbm, fr),
                (t_hbm, t.at[pl.ds(0, FLAT)]), (u_hbm, u.at[pl.ds(0, FLAT)]),
                (k_hbm, kd.at[pl.ds(0, FLAT)]), (v_hbm, v.at[pl.ds(0, FLAT)]),
            )
        )
    ]
    for load in loads:
        load.start()
    barrier = pltpu.get_barrier_semaphore()

    def greet(place):
        pl.semaphore_signal(barrier, inc=1, device_id=at(place), device_id_type=MESH)

    for place in (west, east, north):
        greet(place)

    @pl.when(not_own_e)
    def _():
        greet(north_e)

    @pl.when(not_own_w)
    def _():
        greet(north_w)

    @pl.when(not_bottom)
    def _():
        for place in (south, south_e, south_w):
            greet(place)

    lane8 = lax.broadcasted_iota(jnp.int32, (8, N), 1)
    zero8 = jnp.zeros((8, N), jnp.float32)
    lane = lax.broadcasted_iota(jnp.int32, (NK, N), 1)
    level = lax.broadcasted_iota(jnp.int32, (NK, N), 0).astype(jnp.float32)
    first, last = lane == 0, lane == N - 1

    for k in range(NK + 1):
        p[pl.ds(k * PAD, 8), :] = zero8
        fa[pl.ds(k * PAD, 8), :] = zero8
        fb[pl.ds(k * PAD, 8), :] = zero8

    @pl.when(is_bottom)
    def _():
        recv[SOUTH] = jnp.zeros((MSG, N), jnp.float32)
        crecv[SW] = jnp.zeros((NK, N), jnp.float32)
        crecv[SE] = jnp.zeros((NK, N), jnp.float32)

    def set_cor(b, _):
        rows = pl.ds(pl.multiple_of(b * 8, 8), 8)
        j = lax.broadcasted_iota(jnp.int32, (8, N), 0) + (b * 8 + lat * N)
        cor[rows, :] = 0.25 * jnp.sin(
            jnp.pi * ((j.astype(jnp.float32) + 0.5) / (N * n_lat) - 0.5)
        )
        return 0

    lax.fori_loop(0, N // 8, set_cor, 0)

    for load in loads[:3]:
        load.wait()
    dep[pl.ds(N, 8), :] = zero8
    dep[pl.ds(0, N), :] = (ind[...] * strata[...]).astype(jnp.float32)
    fr[...] = fr[...] * 0.25

    def set_depth(b, _):
        r = pl.multiple_of(b * 8, 8)
        rows = pl.ds(r, 8)
        d = dep[rows, :]
        dep_e[rows, :] = jnp.where(lane8 == N - 1, 0.0, jnp.minimum(d, east_of(d)))
        dep_n[rows, :] = jnp.minimum(d, dep[pl.ds(r + 1, 8), :])
        return 0

    lax.fori_loop(0, N // 8, set_depth, 0, unroll=True)

    def set_columns(place, x):
        y = x.T
        cols[pl.ds(place * 16, 8), :] = y[N - 8 :]
        cols[pl.ds(place * 16 + 8, 8), :] = y[:8]

    set_columns(4 * NK, dep[pl.ds(0, N), :])
    set_columns(4 * NK + 1, fr[...])

    def pack(ref, f, double):
        def step(k, _):
            block = pl.ds(pl.multiple_of(k * N, N), N)
            x = ref[block, :]
            if double:
                x = x + x
                ref[block, :] = x
            set_columns(f * NK + k, x)
            return 0

        lax.fori_loop(0, NK, step, 0, unroll=4)


    def wide(x):
        return jnp.broadcast_to(x, (NK, N))

    def column(f, entry):
        return cols[pl.ds(f * NK * 16 + 6 + entry, NK, stride=16), :]

    def plane_column(i, entry):
        return wide(cols[pl.ds((4 * NK + i) * 16 + 6 + entry, 1), :])

    def columns(entry):
        t_c, u_c, k_c, v_c = (column(f, entry) for f in range(4))
        return t_c, u_c, v_c, k_c, plane_column(0, entry)

    def row(ref, j):
        return ref[pl.ds(j, NK, stride=N), :]

    def edge_rows(j):
        return (
            row(t, j), row(u, j), row(v, j), 2.0 * row(kd, j), wide(dep[pl.ds(j, 1), :]),
        )

    def x_face(a, b):
        return face(level, jnp.minimum(a[4], b[4]), a[1], b[1], a[0], b[0], a[3], b[3])

    def y_face(a, b):
        return face(level, jnp.minimum(a[4], b[4]), a[2], b[2], a[0], b[0], a[3], b[3])

    def closed_step(mid, through, along):
        flow = jnp.where(last, 0.0, along(mid, tuple(east_of(x) for x in mid)))
        tc, _, _, kc, d = mid
        above = jnp.where(
            level + 1.0 < d,
            (kc + pltpu.roll(kc, NK - 1, 0)) * (pltpu.roll(tc, NK - 1, 0) - tc),
            0.0,
        )
        total = through + (west_of(flow) - flow) + (above - pltpu.roll(above, 1, 0))
        return jnp.where(level < d, tc + SCALE * total, 0.0)

    def stage(side, values, tracer):
        for f in range(4):
            send[side, pl.ds(f * NK, NK), :] = values[f]
        send[side, pl.ds(4 * NK, NK), :] = tracer
        send[side, pl.ds(5 * NK, 8), :] = values[4][:8]

    def stage_corners(slab, values):
        x = jnp.zeros((NK, N), jnp.float32)
        for f in range(5):
            x = jnp.where(lane == f, pltpu.roll(values[f], f, 1) if f else values[f], x)
            x = jnp.where(lane == 8 + f, pltpu.roll(values[f], 9 + f, 1), x)
        csend[slab] = x

    for load in loads[3:]:
        load.wait()
    r_n, r_s = edge_rows(N - 1), edge_rows(0)
    stage(NORTH, r_n, closed_step(r_n, y_face(edge_rows(N - 2), r_n), x_face))
    stage(SOUTH, r_s, closed_step(r_s, -y_face(r_s, edge_rows(1)), x_face))
    stage_corners(0, r_n)
    stage_corners(1, r_s)

    pl.semaphore_wait(
        barrier,
        jnp.where(is_bottom, 5, 8) - own_e.astype(jnp.int32) - own_w.astype(jnp.int32),
    )

    def rim(side, slot, place):
        return pltpu.make_async_remote_copy(
            src_ref=send.at[side], dst_ref=recv.at[slot], send_sem=send_sem.at[side],
            recv_sem=recv_sem.at[slot], device_id=at(place), device_id_type=MESH,
        )

    def corner(slab, message, slot, place):
        return pltpu.make_async_remote_copy(
            src_ref=csend.at[slab], dst_ref=crecv.at[slot], send_sem=csend_sem.at[message],
            recv_sem=crecv_sem.at[slot], device_id=at(place), device_id_type=MESH,
        )

    to_north = rim(NORTH, jnp.where(is_top, NORTH, SOUTH), north)
    to_south = rim(SOUTH, NORTH, south)
    to_east, to_west = rim(EAST, WEST, east), rim(WEST, EAST, west)
    to_ne = corner(0, 0, jnp.where(is_top, NE, SW), north_e)
    to_nw = corner(0, 1, jnp.where(is_top, NW, SE), north_w)
    to_se, to_sw = corner(1, 2, NW, south_e), corner(1, 3, NE, south_w)

    to_north.start()

    @pl.when(not_own_e)
    def _():
        to_ne.start()

    @pl.when(not_own_w)
    def _():
        to_nw.start()

    @pl.when(not_bottom)
    def _():
        to_south.start()
        to_se.start()
        to_sw.start()

    for f, ref in enumerate((t, u, kd, v)):
        pack(ref, f, ref is kd)
    c_e, c_w = columns(1), columns(2)
    stage(EAST, c_e, closed_step(c_e, x_face(columns(0), c_e), y_face))
    stage(WEST, c_w, closed_step(c_w, -x_face(c_w, columns(3)), y_face))
    to_east.start()
    to_west.start()

    def tracer(b, _):
        r = pl.multiple_of(b * 8, 8)
        rows = pl.ds(r, 8)
        d, de, dn = dep[rows, :], dep_e[rows, :], dep_n[rows, :]
        below = zero8
        press = zero8
        for k in range(NK):
            c = float(k)
            here, up_rows = pl.ds(r + k * N, 8), pl.ds(r + k * N + 1, 8)
            tc, kc, uc, vc = t[here, :], kd[here, :], u[here, :], v[here, :]
            f_e = face(c, de, uc, east_of(uc), tc, east_of(tc), kc, east_of(kc))
            f_n = face(c, dn, vc, v[up_rows, :], tc, t[up_rows, :], kc, kd[up_rows, :])
            fa[pl.ds(r + k * PAD + 8, 8), :] = f_n
            f_s = fa[pl.ds(r + k * PAD + 7, 8), :]
            if k < NK - 1:
                t_up, k_up = t[pl.ds(r + (k + 1) * N, 8), :], kd[pl.ds(r + (k + 1) * N, 8), :]
                above = jnp.where(c + 1.0 < d, (kc + k_up) * (t_up - tc), 0.0)
            else:
                above = zero8
            total = (west_of(f_e) - f_e) + (f_s - f_n) + (above - below)
            below = above
            tc = jnp.where(c < d, tc + SCALE * total, 0.0)
            tn[here, :] = tc
            press = press + PG * tc
            p[pl.ds(r + k * PAD + 8, 8), :] = press
        return 0

    lax.fori_loop(0, N // 8, tracer, 0)

    def momentum(b, _):
        r = pl.multiple_of(b * 8, 8)
        rows = pl.ds(r, 8)
        d, de, dn = dep[rows, :], dep_e[rows, :], dep_n[rows, :]
        f, co = fr[rows, :], cor[rows, :]
        for k in range(NK):
            c = float(k)
            here, up_rows = pl.ds(r + k * N, 8), pl.ds(r + k * N + 1, 8)
            mine, south_rows = pl.ds(r + k * PAD + 8, 8), pl.ds(r + k * PAD + 7, 8)
            uc, vc, pc = u[here, :], v[here, :], p[mine, :]
            wet_e, wet_n, wet = c < de, c < dn, c < d
            u_e = jnp.where(wet_e, east_of(uc) - uc, 0.0)
            v_e = jnp.where(wet_e, east_of(vc) - vc, 0.0)
            u_n = jnp.where(wet_n, u[up_rows, :] - uc, 0.0)
            v_n = jnp.where(wet_n, v[up_rows, :] - vc, 0.0)
            fa[mine, :] = u_n
            fb[mine, :] = v_n
            lap_u = (u_e - west_of(u_e)) + (u_n - fa[south_rows, :])
            lap_v = (v_e - west_of(v_e)) + (v_n - fb[south_rows, :])
            dp_x = east_of(pc) - west_of(pc)
            dp_y = p[pl.ds(r + k * PAD + 9, 8), :] - p[south_rows, :]
            un[here, :] = jnp.where(wet, (uc + co * vc) - dp_x + f * lap_u, 0.0)
            vn[here, :] = jnp.where(wet, (vc - co * uc) - dp_y + f * lap_v, 0.0)
        return 0

    lax.fori_loop(0, N // 8, momentum, 0)

    rim(NORTH, NORTH, north).wait_recv()
    rim(EAST, EAST, east).wait_recv()
    rim(WEST, WEST, west).wait_recv()

    @pl.when(not_own_e)
    def _():
        corner(0, 0, NE, north_e).wait_recv()

    @pl.when(not_own_w)
    def _():
        corner(0, 1, NW, north_w).wait_recv()

    @pl.when(own_e)
    def _():
        crecv[NE] = csend[0]

    @pl.when(own_w)
    def _():
        crecv[NW] = csend[0]

    @pl.when(not_bottom)
    def _():
        rim(SOUTH, SOUTH, south).wait_recv()
        corner(1, 2, SE, south_e).wait_recv()
        corner(1, 3, SW, south_w).wait_recv()

    @pl.when(is_top)
    def _():
        x = mirrored(recv[NORTH])
        r = lax.broadcasted_iota(jnp.int32, (MSG, N), 0)
        recv[NORTH] = jnp.where((r >= NK) & (r < 3 * NK), -x, x)
        x = pltpu.roll(crecv[NW], 8, 1)
        crecv[NW] = jnp.where((lane == 9) | (lane == 10), -x, x)
        x = pltpu.roll(crecv[NE], N - 8, 1)
        crecv[NE] = jnp.where((lane == 1) | (lane == 2), -x, x)

    def ghost(slot):
        parts = [recv[slot, pl.ds(f * NK, NK), :] for f in range(4)]
        return (*parts, wide(recv[slot, pl.ds(5 * NK, 1), :]))

    def beyond(slot, entry, to):
        x = crecv[slot]
        return tuple(pltpu.roll(x, (to - entry - f) % N, 1) for f in range(5))

    g_w, g_e, g_s, g_n = ghost(WEST), ghost(EAST), ghost(SOUTH), ghost(NORTH)
    f_w, f_e = x_face(g_w, c_w), x_face(c_e, g_e)
    f_s, f_n = y_face(g_s, r_s), y_face(r_n, g_n)

    def whole(slot, flow, low, high):
        ends = jnp.where(first, low, jnp.where(last, high, 0.0))
        return running_sum(PG * (recv[slot, pl.ds(4 * NK, NK), :] + SCALE * (flow + ends)))

    p_w = whole(WEST, -f_w, y_face(beyond(SW, 8, 0), g_w), -y_face(g_w, beyond(NW, 8, N - 1)))
    p_e = whole(EAST, f_e, y_face(beyond(SE, 0, 0), g_e), -y_face(g_e, beyond(NE, 0, N - 1)))
    p_s = whole(SOUTH, -f_s, x_face(beyond(SW, 8, 0), g_s), -x_face(g_s, beyond(SE, 0, N - 1)))
    p_n = whole(NORTH, f_n, x_face(beyond(NW, 8, 0), g_n), -x_face(g_n, beyond(NE, 0, N - 1)))
    t_w, t_e, t_s, t_n = SCALE * f_w, -SCALE * f_e, SCALE * f_s, -SCALE * f_n
    d_w, d_e, d_s, d_n = (running_sum(PG * x) for x in (t_w, t_e, t_s, t_n))
    q_w = running_sum(PG * send[WEST, pl.ds(4 * NK, NK), :])
    q_e = running_sum(PG * send[EAST, pl.ds(4 * NK, NK), :])

    def across(x):
        return jnp.where(first, 0.0, west_of(x)) - jnp.where(last, 0.0, east_of(x))

    def friction(mid, other, f, i):
        m = level < jnp.minimum(mid[4], other[4])
        return jnp.where(m, f * (other[i] - mid[i]), 0.0)

    def masked(depth, x):
        return jnp.where(level < depth, x, 0.0)

    fr_e, fr_w = plane_column(1, 1), plane_column(1, 2)
    fr_s, fr_n = wide(fr[pl.ds(0, 1), :]), wide(fr[pl.ds(N - 1, 1), :])
    def add(ref, j, x):
        rows = pl.ds(j, NK, stride=N)
        ref[rows, :] = ref[rows, :] + x

    add(tn, N - 1, t_n)
    add(tn, 0, t_s)
    add(un, N - 1, friction(r_n, g_n, fr_n, 1) + masked(r_n[4], across(d_n)))
    add(un, 0, friction(r_s, g_s, fr_s, 1) + masked(r_s[4], across(d_s)))
    add(vn, N - 1, friction(r_n, g_n, fr_n, 2) - masked(r_n[4], p_n))
    add(vn, 0, friction(r_s, g_s, fr_s, 2) + masked(r_s[4], p_s))
    add(vn, N - 2, -masked(wide(dep[pl.ds(N - 2, 1), :]), d_n))
    add(vn, 1, masked(wide(dep[pl.ds(1, 1), :]), d_s))
    fix[pl.ds(0, NK, stride=4), :] = -masked(plane_column(0, 0), d_e)
    fix[pl.ds(1, NK, stride=4), :] = friction(c_e, g_e, fr_e, 1) - masked(c_e[4], p_e - q_w)
    fix[pl.ds(2, NK, stride=4), :] = friction(c_w, g_w, fr_w, 1) + masked(c_w[4], p_w - q_e)
    fix[pl.ds(3, NK, stride=4), :] = masked(plane_column(0, 3), d_w)
    fix[pl.ds(64, NK, stride=2), :] = friction(c_e, g_e, fr_e, 2) + masked(c_e[4], across(d_e))
    fix[pl.ds(65, NK, stride=2), :] = friction(c_w, g_w, fr_w, 2) + masked(c_w[4], across(d_w))
    fix[pl.ds(96, NK, stride=2), :] = t_e
    fix[pl.ds(97, NK, stride=2), :] = t_w
    fix[...] = fix[...].T
    rim2 = (lane8 == 0) | (lane8 == N - 1)
    rim4 = (lane8 <= 1) | (lane8 >= N - 2)

    def finish(b, _):
        r = pl.multiple_of(b * 8, 8)
        x = fix[pl.ds(r, 8), :]
        for k in range(NK):
            here = pl.ds(r + k * N, 8)
            un[here, :] = un[here, :] + jnp.where(rim4, pltpu.roll(x, N - 2 - 4 * k, 1), 0.0)
            vn[here, :] = vn[here, :] + jnp.where(rim2, pltpu.roll(x, 63 - 2 * k, 1), 0.0)
            tn[here, :] = tn[here, :] + jnp.where(rim2, pltpu.roll(x, 31 - 2 * k, 1), 0.0)
        return 0

    lax.fori_loop(0, N // 8, finish, 0, unroll=2)

    to_north.wait_send()
    to_east.wait_send()
    to_west.wait_send()

    @pl.when(not_own_e)
    def _():
        to_ne.wait_send()

    @pl.when(not_own_w)
    def _():
        to_nw.wait_send()

    @pl.when(not_bottom)
    def _():
        to_south.wait_send()
        to_se.wait_send()
        to_sw.wait_send()


def solution(mesh):
    n_lon, n_lat = mesh.shape["lon"], mesh.shape["lat"]
    f32, i32 = jnp.float32, jnp.int32

    def on_device(t, u, v, kd, fr, ind, strata):
        flat = [x.reshape(FLAT, N) for x in (t, u, v, kd)]
        outs = pl.pallas_call(
            functools.partial(kernel, n_lon, n_lat),
            out_shape=[pltpu.VMEM((FLAT, N), f32)] * 3,
            in_specs=[pl.BlockSpec(memory_space=pltpu.HBM)] * 7,
            out_specs=[pl.BlockSpec(memory_space=pltpu.VMEM)] * 3,
            scratch_shapes=[
                *[pltpu.VMEM((FLAT + 8, N), f32)] * 4,
                *[pltpu.VMEM((NK * PAD + 8, N), f32)] * 3,
                pltpu.VMEM((N, N), f32),
                pltpu.VMEM((N, N), i32),
                pltpu.VMEM((N, N), i32),
                pltpu.VMEM((N + 8, N), f32),
                *[pltpu.VMEM((N, N), f32)] * 3,
                pltpu.VMEM(((4 * NK + 2) * 16, N), f32),
                pltpu.VMEM((N, N), f32),
                pltpu.VMEM((4, MSG, N), f32),
                pltpu.VMEM((4, MSG, N), f32),
                pltpu.VMEM((4, NK, N), f32),
                pltpu.VMEM((4, NK, N), f32),
                pltpu.SemaphoreType.DMA((7,)),
                *[pltpu.SemaphoreType.DMA((4,))] * 4,
            ],
            compiler_params=pltpu.CompilerParams(
                collective_id=0, has_side_effects=True, vmem_limit_bytes=60 * 1024 * 1024
            ),
            cost_estimate=pl.CostEstimate(
                flops=80 * FLAT * N, bytes_accessed=30 * FLAT * N, transcendentals=0
            ),
        )(*flat, fr, ind, strata)
        return tuple(x.reshape(NK, N, N) for x in outs)

    plane, field = P("lat", "lon"), P(None, "lat", "lon")
    return jax.shard_map(
        on_device,
        mesh=mesh,
        in_specs=(field, field, field, field, plane, plane, plane),
        out_specs=(field, field, field),
        check_vma=False,
    )
```

time: 26.9 us -> 22.6 us (0.84)
  the two profiles are of different devices: /device:TPU:23 before, /device:TPU:6 now
where the time goes in v2:
time: 22.6 us; the launch traced here: 22.5 us
  Pallas kernels  18.9 us (84%)
  local copies, waits for them, and re-layouts  2.91 us (13%)
  between operations  0.64 us (3%)
    pallas_call x1, Pallas kernels, on_device(): pl.pallas_call(functools.partial(kernel, n_lon, n_lat), out_shape=[pltpu....  18.9 us
    unnamed x3, local copies, waits for them, and re-layouts  2.91 us

profile of v2, /device:TPU:6, one launch (start us, length us, event | category | flops | bytes accessed | tf_op | source)
XLA Modules:
  0.0 22.5 jit_solution(8790777970175765841)
XLA Ops:
  0.6 18.9 %shard_map.94 = (f32[2048,128]{1,0:T(8,128)S(1)}, f32[2048,128]{1,0:T(8,128)S(1)}, f32[2048,128]{1,0:T(8,128)S(1)}) custom-call(f32[2048,128]{1,0:T(8,128)} %bitcast.10, f32[2048,128]{1,0:T(8,128)} %bitcast.11, f32[2048,128]{1,0:T(8,128)} %bitcast.12, f32[2048,128]{1,0:T(8,128)} %bitcast.13, f32[128,128]{1,0:T(8,128)} %fr_hbm.1, s32[128,128]{1,0:T(8,128)} %ind_hbm.1, ...), custom_call_target="tpu_custom_call" | custom-call | flops 20971520 | bytes 7864320 | tf_op jit(solution)/shard_map/pallas_call | solution.py:469
  19.6 1.0 %copy.13 = f32[16,128,128]{2,1,0:T(8,128)} copy(f32[16,128,128]{2,1,0:T(8,128)S(1)} %bitcast.9) | data formatting | bytes 2097152
  20.6 1.0 %copy.14 = f32[16,128,128]{2,1,0:T(8,128)} copy(f32[16,128,128]{2,1,0:T(8,128)S(1)} %bitcast.8) | data formatting | bytes 2097152
  21.5 1.0 %copy.15 = f32[16,128,128]{2,1,0:T(8,128)} copy(f32[16,128,128]{2,1,0:T(8,128)S(1)} %bitcast.7) | data formatting | bytes 2097152

commit v3 on v2

--- a/solution.py
+++ b/solution.py
@@ -49,9 +49,9 @@
 def kernel(
     n_lon, n_lat,
     t_hbm, u_hbm, v_hbm, k_hbm, fr_hbm, ind_hbm, str_hbm,
-    tn, un, vn,
-    t, u, v, kd, p, fa, fb, fr, ind, strata, dep, dep_e, dep_n, cor,
-    cols, fix, send, recv, csend, crecv,
+    tn, un, vn, fix_out,
+    t, u, v, kd, p, fa, fb, fr, ind, strata, dep, dep_e, dep_n, cor, fr_e,
+    ue, cols, fix, send, recv, csend, crecv,
     in_sem, send_sem, recv_sem, csend_sem, crecv_sem,
 ):
     lon, lat = lax.axis_index("lon"), lax.axis_index("lat")
@@ -144,6 +144,7 @@
         d = dep[rows, :]
         dep_e[rows, :] = jnp.where(lane8 == N - 1, 0.0, jnp.minimum(d, east_of(d)))
         dep_n[rows, :] = jnp.minimum(d, dep[pl.ds(r + 1, 8), :])
+        fr_e[rows, :] = east_of(fr[rows, :])
         return 0
 
     lax.fori_loop(0, N // 8, set_depth, 0, unroll=True)
@@ -286,7 +287,9 @@
             c = float(k)
             here, up_rows = pl.ds(r + k * N, 8), pl.ds(r + k * N + 1, 8)
             tc, kc, uc, vc = t[here, :], kd[here, :], u[here, :], v[here, :]
-            f_e = face(c, de, uc, east_of(uc), tc, east_of(tc), kc, east_of(kc))
+            next_u = east_of(uc)
+            ue[here, :] = next_u
+            f_e = face(c, de, uc, next_u, tc, east_of(tc), kc, east_of(kc))
             f_n = face(c, dn, vc, v[up_rows, :], tc, t[up_rows, :], kc, kd[up_rows, :])
             fa[pl.ds(r + k * PAD + 8, 8), :] = f_n
             f_s = fa[pl.ds(r + k * PAD + 7, 8), :]
@@ -303,30 +306,31 @@
             p[pl.ds(r + k * PAD + 8, 8), :] = press
         return 0
 
-    lax.fori_loop(0, N // 8, tracer, 0)
+    lax.fori_loop(0, N // 8, tracer, 0, unroll=2)
 
     def momentum(b, _):
         r = pl.multiple_of(b * 8, 8)
         rows = pl.ds(r, 8)
         d, de, dn = dep[rows, :], dep_e[rows, :], dep_n[rows, :]
-        f, co = fr[rows, :], cor[rows, :]
+        f, f_next, co = fr[rows, :], fr_e[rows, :], cor[rows, :]
         for k in range(NK):
             c = float(k)
             here, up_rows = pl.ds(r + k * N, 8), pl.ds(r + k * N + 1, 8)
             mine, south_rows = pl.ds(r + k * PAD + 8, 8), pl.ds(r + k * PAD + 7, 8)
             uc, vc, pc = u[here, :], v[here, :], p[mine, :]
             wet_e, wet_n, wet = c < de, c < dn, c < d
-            u_e = jnp.where(wet_e, east_of(uc) - uc, 0.0)
+            u_e = jnp.where(wet_e, ue[here, :] - uc, 0.0)
             v_e = jnp.where(wet_e, east_of(vc) - vc, 0.0)
             u_n = jnp.where(wet_n, u[up_rows, :] - uc, 0.0)
             v_n = jnp.where(wet_n, v[up_rows, :] - vc, 0.0)
             fa[mine, :] = u_n
             fb[mine, :] = v_n
-            lap_u = (u_e - west_of(u_e)) + (u_n - fa[south_rows, :])
+            gain = east_of(pc) - pc
+            across_x = (f * u_e - gain) - west_of(gain + f_next * u_e)
+            lap_u = u_n - fa[south_rows, :]
             lap_v = (v_e - west_of(v_e)) + (v_n - fb[south_rows, :])
-            dp_x = east_of(pc) - west_of(pc)
             dp_y = p[pl.ds(r + k * PAD + 9, 8), :] - p[south_rows, :]
-            un[here, :] = jnp.where(wet, (uc + co * vc) - dp_x + f * lap_u, 0.0)
+            un[here, :] = jnp.where(wet, (uc + co * vc) + across_x + f * lap_u, 0.0)
             vn[here, :] = jnp.where(wet, (vc - co * uc) - dp_y + f * lap_v, 0.0)
         return 0
 
@@ -403,43 +407,29 @@
     def masked(depth, x):
         return jnp.where(level < depth, x, 0.0)
 
-    fr_e, fr_w = plane_column(1, 1), plane_column(1, 2)
-    fr_s, fr_n = wide(fr[pl.ds(0, 1), :]), wide(fr[pl.ds(N - 1, 1), :])
+    col_e, col_w = plane_column(1, 1), plane_column(1, 2)
+    row_s, row_n = wide(fr[pl.ds(0, 1), :]), wide(fr[pl.ds(N - 1, 1), :])
     def add(ref, j, x):
         rows = pl.ds(j, NK, stride=N)
         ref[rows, :] = ref[rows, :] + x
 
     add(tn, N - 1, t_n)
     add(tn, 0, t_s)
-    add(un, N - 1, friction(r_n, g_n, fr_n, 1) + masked(r_n[4], across(d_n)))
-    add(un, 0, friction(r_s, g_s, fr_s, 1) + masked(r_s[4], across(d_s)))
-    add(vn, N - 1, friction(r_n, g_n, fr_n, 2) - masked(r_n[4], p_n))
-    add(vn, 0, friction(r_s, g_s, fr_s, 2) + masked(r_s[4], p_s))
+    add(un, N - 1, friction(r_n, g_n, row_n, 1) + masked(r_n[4], across(d_n)))
+    add(un, 0, friction(r_s, g_s, row_s, 1) + masked(r_s[4], across(d_s)))
+    add(vn, N - 1, friction(r_n, g_n, row_n, 2) - masked(r_n[4], p_n))
+    add(vn, 0, friction(r_s, g_s, row_s, 2) + masked(r_s[4], p_s))
     add(vn, N - 2, -masked(wide(dep[pl.ds(N - 2, 1), :]), d_n))
     add(vn, 1, masked(wide(dep[pl.ds(1, 1), :]), d_s))
     fix[pl.ds(0, NK, stride=4), :] = -masked(plane_column(0, 0), d_e)
-    fix[pl.ds(1, NK, stride=4), :] = friction(c_e, g_e, fr_e, 1) - masked(c_e[4], p_e - q_w)
-    fix[pl.ds(2, NK, stride=4), :] = friction(c_w, g_w, fr_w, 1) + masked(c_w[4], p_w - q_e)
+    fix[pl.ds(1, NK, stride=4), :] = friction(c_e, g_e, col_e, 1) - masked(c_e[4], p_e - q_w)
+    fix[pl.ds(2, NK, stride=4), :] = friction(c_w, g_w, col_w, 1) + masked(c_w[4], p_w - q_e)
     fix[pl.ds(3, NK, stride=4), :] = masked(plane_column(0, 3), d_w)
-    fix[pl.ds(64, NK, stride=2), :] = friction(c_e, g_e, fr_e, 2) + masked(c_e[4], across(d_e))
-    fix[pl.ds(65, NK, stride=2), :] = friction(c_w, g_w, fr_w, 2) + masked(c_w[4], across(d_w))
+    fix[pl.ds(64, NK, stride=2), :] = friction(c_e, g_e, col_e, 2) + masked(c_e[4], across(d_e))
+    fix[pl.ds(65, NK, stride=2), :] = friction(c_w, g_w, col_w, 2) + masked(c_w[4], across(d_w))
     fix[pl.ds(96, NK, stride=2), :] = t_e
     fix[pl.ds(97, NK, stride=2), :] = t_w
-    fix[...] = fix[...].T
-    rim2 = (lane8 == 0) | (lane8 == N - 1)
-    rim4 = (lane8 <= 1) | (lane8 >= N - 2)
-
-    def finish(b, _):
-        r = pl.multiple_of(b * 8, 8)
-        x = fix[pl.ds(r, 8), :]
-        for k in range(NK):
-            here = pl.ds(r + k * N, 8)
-            un[here, :] = un[here, :] + jnp.where(rim4, pltpu.roll(x, N - 2 - 4 * k, 1), 0.0)
-            vn[here, :] = vn[here, :] + jnp.where(rim2, pltpu.roll(x, 63 - 2 * k, 1), 0.0)
-            tn[here, :] = tn[here, :] + jnp.where(rim2, pltpu.roll(x, 31 - 2 * k, 1), 0.0)
-        return 0
-
-    lax.fori_loop(0, N // 8, finish, 0, unroll=2)
+    fix_out[...] = fix[...].T
 
     to_north.wait_send()
     to_east.wait_send()
@@ -458,6 +448,40 @@
         to_south.wait_send()
         to_se.wait_send()
         to_sw.wait_send()
+
+
+def finish(tn, un, vn, fix, t_out, u_out, v_out, t, u, v, out_sem):
+    lane8 = lax.broadcasted_iota(jnp.int32, (8, N), 1)
+    rim2 = (lane8 == 0) | (lane8 == N - 1)
+    rim4 = (lane8 <= 1) | (lane8 >= N - 2)
+
+    def copies(k):
+        block = pl.ds(pl.multiple_of(k * N, N), N)
+        return [
+            pltpu.make_async_copy(src.at[block], dst.at[block], out_sem.at[i, k])
+            for i, (src, dst) in enumerate(((t, t_out), (u, u_out), (v, v_out)))
+        ]
+
+    def level(k, _):
+        for r in range(0, N, 8):
+            here = pl.ds(pl.multiple_of(k * N + r, 8), 8)
+            x = fix[pl.ds(r, 8), :]
+            for new, old, rim, shift in (
+                (u, un, rim4, N - 2 - 4 * k), (v, vn, rim2, 63 - 2 * k), (t, tn, rim2, 31 - 2 * k),
+            ):
+                new[here, :] = old[here, :] + jnp.where(rim, pltpu.roll(x, shift, 1), 0.0)
+        for copy in copies(k):
+            copy.start()
+        return 0
+
+    lax.fori_loop(0, NK, level, 0)
+
+    def drain(k, _):
+        for copy in copies(k):
+            copy.wait()
+        return 0
+
+    lax.fori_loop(0, NK, drain, 0)
 
 
 def solution(mesh):
@@ -468,9 +492,9 @@
         flat = [x.reshape(FLAT, N) for x in (t, u, v, kd)]
         outs = pl.pallas_call(
             functools.partial(kernel, n_lon, n_lat),
-            out_shape=[pltpu.VMEM((FLAT, N), f32)] * 3,
+            out_shape=[*[pltpu.VMEM((FLAT, N), f32)] * 3, pltpu.VMEM((N, N), f32)],
             in_specs=[pl.BlockSpec(memory_space=pltpu.HBM)] * 7,
-            out_specs=[pl.BlockSpec(memory_space=pltpu.VMEM)] * 3,
+            out_specs=[pl.BlockSpec(memory_space=pltpu.VMEM)] * 4,
             scratch_shapes=[
                 *[pltpu.VMEM((FLAT + 8, N), f32)] * 4,
                 *[pltpu.VMEM((NK * PAD + 8, N), f32)] * 3,
@@ -478,7 +502,8 @@
                 pltpu.VMEM((N, N), i32),
                 pltpu.VMEM((N, N), i32),
                 pltpu.VMEM((N + 8, N), f32),
-                *[pltpu.VMEM((N, N), f32)] * 3,
+                *[pltpu.VMEM((N, N), f32)] * 4,
+                pltpu.VMEM((FLAT, N), f32),
                 pltpu.VMEM(((4 * NK + 2) * 16, N), f32),
                 pltpu.VMEM((N, N), f32),
                 pltpu.VMEM((4, MSG, N), f32),
@@ -495,6 +520,17 @@
                 flops=80 * FLAT * N, bytes_accessed=30 * FLAT * N, transcendentals=0
             ),
         )(*flat, fr, ind, strata)
+        outs = pl.pallas_call(
+            finish,
+            out_shape=[jax.ShapeDtypeStruct((FLAT, N), f32)] * 3,
+            in_specs=[pl.BlockSpec(memory_space=pltpu.VMEM)] * 4,
+            out_specs=[pl.BlockSpec(memory_space=pltpu.HBM)] * 3,
+            scratch_shapes=[
+                *[pltpu.VMEM((FLAT, N), f32)] * 3,
+                pltpu.SemaphoreType.DMA((3, NK)),
+            ],
+            compiler_params=pltpu.CompilerParams(vmem_limit_bytes=32 * 1024 * 1024),
+        )(*outs)
         return tuple(x.reshape(NK, N, N) for x in outs)
 
     plane, field = P("lat", "lon"), P(None, "lat", "lon")

time: 22.6 us -> 20.2 us (0.89)
  local copies, waits for them, and re-layouts: 2.91 us -> 0 us
  Pallas kernels: 18.9 us -> 19.5 us
    unnamed x3 -> x0, local copies, waits for them, and re-layouts: 2.91 us -> none
    pallas_call x1 -> x2, Pallas kernels: 18.9 us -> 19.5 us  [the longest x1 16.5 us: on_device(): pl.pallas_call(functools.partial(kernel, n_lon, n_lat), out_shape=[*[pltp...]
where the time goes in v3:
time: 20.2 us; the launch traced here: 20.1 us
  Pallas kernels  19.5 us (97%)
  between operations  0.64 us (3%)
    pallas_call x1, Pallas kernels, on_device(): pl.pallas_call(functools.partial(kernel, n_lon, n_lat), out_shape=[*[pltp...  16.5 us
    pallas_call x1, Pallas kernels, on_device(): pl.pallas_call(finish, out_shape=[jax.ShapeDtypeStruct((FLAT, N), f32)] *...  3.01 us

profile of v3, /device:TPU:6, one launch (start us, length us, event | category | flops | bytes accessed | tf_op | source)
XLA Modules:
  0.0 20.1 jit_solution(6241240342357962105)
XLA Ops:
  0.6 16.5 %shard_map.94 = (f32[2048,128]{1,0:T(8,128)S(1)}, f32[2048,128]{1,0:T(8,128)S(1)}, f32[2048,128]{1,0:T(8,128)S(1)}, f32[128,128]{1,0:T(8,128)S(1)}) custom-call(f32[2048,128]{1,0:T(8,128)} %bitcast.7, f32[2048,128]{1,0:T(8,128)} %bitcast.8, f32[2048,128]{1,0:T(8,128)} %bitcast.9, f32[2048,128]{1,0:T(8,128)} %bitcast.10, f32[128,128]{1,0:T(8,128)} %fr_hbm.1, ...), custom_call_target="tpu_custom_call" | custom-call | flops 20971520 | bytes 7864320 | tf_op jit(solution)/shard_map/pallas_call | solution.py:493
  17.1 3.0 %shard_map.95 = (f32[2048,128]{1,0:T(8,128)}, f32[2048,128]{1,0:T(8,128)}, f32[2048,128]{1,0:T(8,128)}) custom-call(f32[2048,128]{1,0:T(8,128)S(1)} %get-tuple-element.10.tn, f32[2048,128]{1,0:T(8,128)S(1)} %get-tuple-element.11.un, f32[2048,128]{1,0:T(8,128)S(1)} %get-tuple-element.12.vn, f32[128,128]{1,0:T(8,128)S(1)} %get-tuple-element.13.fix), custom_call_target="tpu_custom_call" | custom-call | tf_op jit(solution)/shard_map/pallas_call | solution.py:523

commit v4 on v3

--- a/solution.py
+++ b/solution.py
@@ -18,6 +18,7 @@
 WEST, EAST, SOUTH, NORTH = 0, 1, 2, 3
 SW, SE, NW, NE = 0, 1, 2, 3
 MSG = 5 * NK + 8
+CHUNK = 4
 
 
 def east_of(x):
@@ -167,7 +168,7 @@
             set_columns(f * NK + k, x)
             return 0
 
-        lax.fori_loop(0, NK, step, 0, unroll=4)
+        lax.fori_loop(0, NK, step, 0, unroll=8)
 
 
     def wide(x):
@@ -229,6 +230,12 @@
     stage_corners(0, r_n)
     stage_corners(1, r_s)
 
+    for f, ref in enumerate((t, u, kd, v)):
+        pack(ref, f, ref is kd)
+    c_e, c_w = columns(1), columns(2)
+    stage(EAST, c_e, closed_step(c_e, x_face(columns(0), c_e), y_face))
+    stage(WEST, c_w, closed_step(c_w, -x_face(c_w, columns(3)), y_face))
+
     pl.semaphore_wait(
         barrier,
         jnp.where(is_bottom, 5, 8) - own_e.astype(jnp.int32) - own_w.astype(jnp.int32),
@@ -269,11 +276,6 @@
         to_se.start()
         to_sw.start()
 
-    for f, ref in enumerate((t, u, kd, v)):
-        pack(ref, f, ref is kd)
-    c_e, c_w = columns(1), columns(2)
-    stage(EAST, c_e, closed_step(c_e, x_face(columns(0), c_e), y_face))
-    stage(WEST, c_w, closed_step(c_w, -x_face(c_w, columns(3)), y_face))
     to_east.start()
     to_west.start()
 
@@ -455,33 +457,27 @@
     rim2 = (lane8 == 0) | (lane8 == N - 1)
     rim4 = (lane8 <= 1) | (lane8 >= N - 2)
 
-    def copies(k):
-        block = pl.ds(pl.multiple_of(k * N, N), N)
-        return [
-            pltpu.make_async_copy(src.at[block], dst.at[block], out_sem.at[i, k])
-            for i, (src, dst) in enumerate(((t, t_out), (u, u_out), (v, v_out)))
-        ]
-
-    def level(k, _):
-        for r in range(0, N, 8):
-            here = pl.ds(pl.multiple_of(k * N + r, 8), 8)
-            x = fix[pl.ds(r, 8), :]
-            for new, old, rim, shift in (
-                (u, un, rim4, N - 2 - 4 * k), (v, vn, rim2, 63 - 2 * k), (t, tn, rim2, 31 - 2 * k),
-            ):
-                new[here, :] = old[here, :] + jnp.where(rim, pltpu.roll(x, shift, 1), 0.0)
-        for copy in copies(k):
-            copy.start()
+    outs = ((t, t_out), (u, u_out), (v, v_out))
+
+    def step(g, _):
+        for k in range(CHUNK):
+            start = pl.multiple_of((g * CHUNK + k) * N, N)
+            for r in range(0, N, 8):
+                here = pl.ds(start + r, 8)
+                x = fix[pl.ds(r, 8), :]
+                for new, old, rim, shift in (
+                    (u, un, rim4, N - 2 - 4 * k), (v, vn, rim2, 63 - 2 * k), (t, tn, rim2, 31 - 2 * k),
+                ):
+                    shift = lax.rem(shift + N - g * CHUNK * (4 if rim is rim4 else 2), N)
+                    new[here, :] = old[here, :] + jnp.where(rim, pltpu.roll(x, shift, 1), 0.0)
+        block = pl.ds(pl.multiple_of(g * CHUNK * N, N), CHUNK * N)
+        for i, (src, dst) in enumerate(outs):
+            pltpu.make_async_copy(src.at[block], dst.at[block], out_sem.at[i]).start()
         return 0
 
-    lax.fori_loop(0, NK, level, 0)
-
-    def drain(k, _):
-        for copy in copies(k):
-            copy.wait()
-        return 0
-
-    lax.fori_loop(0, NK, drain, 0)
+    lax.fori_loop(0, NK // CHUNK, step, 0)
+    for i, (src, dst) in enumerate(outs):
+        pltpu.make_async_copy(src, dst, out_sem.at[i]).wait()
 
 
 def solution(mesh):
@@ -527,7 +523,7 @@
             out_specs=[pl.BlockSpec(memory_space=pltpu.HBM)] * 3,
             scratch_shapes=[
                 *[pltpu.VMEM((FLAT, N), f32)] * 3,
-                pltpu.SemaphoreType.DMA((3, NK)),
+                pltpu.SemaphoreType.DMA((3,)),
             ],
             compiler_params=pltpu.CompilerParams(vmem_limit_bytes=32 * 1024 * 1024),
         )(*outs)

time: 20.2 us -> 18.4 us (0.911)
  Pallas kernels: 19.5 us -> 17.5 us
    pallas_call x1, Pallas kernels: 3.01 us -> 1.98 us  [on_device(): pl.pallas_call(finish, out_shape=[jax.ShapeDtypeStruct((FLAT, N), f32)] *...]
    pallas_call x1, Pallas kernels: 16.5 us -> 15.5 us  [on_device(): pl.pallas_call(functools.partial(kernel, n_lon, n_lat), out_shape=[*[pltp...]
where the time goes in v4:
time: 18.4 us; the launch traced here: 18.1 us
  Pallas kernels  17.5 us (95%)
  between operations  0.64 us (3%)
    pallas_call x1, Pallas kernels, on_device(): pl.pallas_call(functools.partial(kernel, n_lon, n_lat), out_shape=[*[pltp...  15.5 us
    pallas_call x1, Pallas kernels, on_device(): pl.pallas_call(finish, out_shape=[jax.ShapeDtypeStruct((FLAT, N), f32)] *...  1.98 us

profile of v4, /device:TPU:6, one launch (start us, length us, event | category | flops | bytes accessed | tf_op | source)
XLA Modules:
  0.0 18.1 jit_solution(4367016707905028750)
XLA Ops:
  0.6 15.5 %shard_map.94 = (f32[2048,128]{1,0:T(8,128)S(1)}, f32[2048,128]{1,0:T(8,128)S(1)}, f32[2048,128]{1,0:T(8,128)S(1)}, f32[128,128]{1,0:T(8,128)S(1)}) custom-call(f32[2048,128]{1,0:T(8,128)} %bitcast.7, f32[2048,128]{1,0:T(8,128)} %bitcast.8, f32[2048,128]{1,0:T(8,128)} %bitcast.9, f32[2048,128]{1,0:T(8,128)} %bitcast.10, f32[128,128]{1,0:T(8,128)} %fr_hbm.1, ...), custom_call_target="tpu_custom_call" | custom-call | flops 20971520 | bytes 7864320 | tf_op jit(solution)/shard_map/pallas_call | solution.py:489
  16.1 2.0 %shard_map.95 = (f32[2048,128]{1,0:T(8,128)}, f32[2048,128]{1,0:T(8,128)}, f32[2048,128]{1,0:T(8,128)}) custom-call(f32[2048,128]{1,0:T(8,128)S(1)} %get-tuple-element.10.tn, f32[2048,128]{1,0:T(8,128)S(1)} %get-tuple-element.11.un, f32[2048,128]{1,0:T(8,128)S(1)} %get-tuple-element.12.vn, f32[128,128]{1,0:T(8,128)S(1)} %get-tuple-element.13.fix), custom_call_target="tpu_custom_call" | custom-call | tf_op jit(solution)/shard_map/pallas_call | solution.py:519

commit v5 on v4

--- a/solution.py
+++ b/solution.py
@@ -189,7 +189,7 @@
 
     def edge_rows(j):
         return (
-            row(t, j), row(u, j), row(v, j), 2.0 * row(kd, j), wide(dep[pl.ds(j, 1), :]),
+            row(t, j), row(u, j), row(v, j), row(kd, j), wide(dep[pl.ds(j, 1), :]),
         )
 
     def x_face(a, b):
@@ -222,62 +222,15 @@
             x = jnp.where(lane == 8 + f, pltpu.roll(values[f], 9 + f, 1), x)
         csend[slab] = x
 
-    for load in loads[3:]:
-        load.wait()
+    for f, ref in enumerate((t, u, kd)):
+        loads[3 + f].wait()
+        pack(ref, f, ref is kd)
+    loads[6].wait()
     r_n, r_s = edge_rows(N - 1), edge_rows(0)
     stage(NORTH, r_n, closed_step(r_n, y_face(edge_rows(N - 2), r_n), x_face))
     stage(SOUTH, r_s, closed_step(r_s, -y_face(r_s, edge_rows(1)), x_face))
     stage_corners(0, r_n)
     stage_corners(1, r_s)
-
-    for f, ref in enumerate((t, u, kd, v)):
-        pack(ref, f, ref is kd)
-    c_e, c_w = columns(1), columns(2)
-    stage(EAST, c_e, closed_step(c_e, x_face(columns(0), c_e), y_face))
-    stage(WEST, c_w, closed_step(c_w, -x_face(c_w, columns(3)), y_face))
-
-    pl.semaphore_wait(
-        barrier,
-        jnp.where(is_bottom, 5, 8) - own_e.astype(jnp.int32) - own_w.astype(jnp.int32),
-    )
-
-    def rim(side, slot, place):
-        return pltpu.make_async_remote_copy(
-            src_ref=send.at[side], dst_ref=recv.at[slot], send_sem=send_sem.at[side],
-            recv_sem=recv_sem.at[slot], device_id=at(place), device_id_type=MESH,
-        )
-
-    def corner(slab, message, slot, place):
-        return pltpu.make_async_remote_copy(
-            src_ref=csend.at[slab], dst_ref=crecv.at[slot], send_sem=csend_sem.at[message],
-            recv_sem=crecv_sem.at[slot], device_id=at(place), device_id_type=MESH,
-        )
-
-    to_north = rim(NORTH, jnp.where(is_top, NORTH, SOUTH), north)
-    to_south = rim(SOUTH, NORTH, south)
-    to_east, to_west = rim(EAST, WEST, east), rim(WEST, EAST, west)
-    to_ne = corner(0, 0, jnp.where(is_top, NE, SW), north_e)
-    to_nw = corner(0, 1, jnp.where(is_top, NW, SE), north_w)
-    to_se, to_sw = corner(1, 2, NW, south_e), corner(1, 3, NE, south_w)
-
-    to_north.start()
-
-    @pl.when(not_own_e)
-    def _():
-        to_ne.start()
-
-    @pl.when(not_own_w)
-    def _():
-        to_nw.start()
-
-    @pl.when(not_bottom)
-    def _():
-        to_south.start()
-        to_se.start()
-        to_sw.start()
-
-    to_east.start()
-    to_west.start()
 
     def tracer(b, _):
         r = pl.multiple_of(b * 8, 8)
@@ -308,7 +261,62 @@
             p[pl.ds(r + k * PAD + 8, 8), :] = press
         return 0
 
-    lax.fori_loop(0, N // 8, tracer, 0, unroll=2)
+    ahead = lax.rem(lon, n_lon // 2) < 3 * n_lon // 16
+
+    @pl.when(ahead)
+    def _():
+        lax.fori_loop(0, N // 8, tracer, 0, unroll=2)
+
+    pl.semaphore_wait(
+        barrier,
+        jnp.where(is_bottom, 5, 8) - own_e.astype(jnp.int32) - own_w.astype(jnp.int32),
+    )
+
+    def rim(side, slot, place):
+        return pltpu.make_async_remote_copy(
+            src_ref=send.at[side], dst_ref=recv.at[slot], send_sem=send_sem.at[side],
+            recv_sem=recv_sem.at[slot], device_id=at(place), device_id_type=MESH,
+        )
+
+    def corner(slab, message, slot, place):
+        return pltpu.make_async_remote_copy(
+            src_ref=csend.at[slab], dst_ref=crecv.at[slot], send_sem=csend_sem.at[message],
+            recv_sem=crecv_sem.at[slot], device_id=at(place), device_id_type=MESH,
+        )
+
+    to_north = rim(NORTH, jnp.where(is_top, NORTH, SOUTH), north)
+    to_south = rim(SOUTH, NORTH, south)
+    to_east, to_west = rim(EAST, WEST, east), rim(WEST, EAST, west)
+    to_ne = corner(0, 0, jnp.where(is_top, NE, SW), north_e)
+    to_nw = corner(0, 1, jnp.where(is_top, NW, SE), north_w)
+    to_se, to_sw = corner(1, 2, NW, south_e), corner(1, 3, NE, south_w)
+
+    to_north.start()
+
+    @pl.when(not_own_e)
+    def _():
+        to_ne.start()
+
+    @pl.when(not_own_w)
+    def _():
+        to_nw.start()
+
+    @pl.when(not_bottom)
+    def _():
+        to_south.start()
+        to_se.start()
+        to_sw.start()
+
+    pack(v, 3, False)
+    c_e, c_w = columns(1), columns(2)
+    stage(EAST, c_e, closed_step(c_e, x_face(columns(0), c_e), y_face))
+    stage(WEST, c_w, closed_step(c_w, -x_face(c_w, columns(3)), y_face))
+    to_east.start()
+    to_west.start()
+
+    @pl.when(jnp.logical_not(ahead))
+    def _():
+        lax.fori_loop(0, N // 8, tracer, 0, unroll=2)
 
     def momentum(b, _):
         r = pl.multiple_of(b * 8, 8)

time: 18.4 us -> 17 us (0.924)
  the two profiles are of different devices: /device:TPU:6 before, /device:TPU:7 now
where the time goes in v5:
time: 17 us; the launch traced here: 16.9 us
  Pallas kernels  16.2 us (95%)
  between operations  0.64 us (4%)
    pallas_call x1, Pallas kernels, on_device(): pl.pallas_call(functools.partial(kernel, n_lon, n_lat), out_shape=[*[pltp...  14.2 us
    pallas_call x1, Pallas kernels, on_device(): pl.pallas_call(finish, out_shape=[jax.ShapeDtypeStruct((FLAT, N), f32)] *...  1.98 us

profile of v5, /device:TPU:7, one launch (start us, length us, event | category | flops | bytes accessed | tf_op | source)
XLA Modules:
  0.0 16.9 jit_solution(9116256688720852762)
XLA Ops:
  0.6 14.2 %shard_map.94 = (f32[2048,128]{1,0:T(8,128)S(1)}, f32[2048,128]{1,0:T(8,128)S(1)}, f32[2048,128]{1,0:T(8,128)S(1)}, f32[128,128]{1,0:T(8,128)S(1)}) custom-call(f32[2048,128]{1,0:T(8,128)} %bitcast.7, f32[2048,128]{1,0:T(8,128)} %bitcast.8, f32[2048,128]{1,0:T(8,128)} %bitcast.9, f32[2048,128]{1,0:T(8,128)} %bitcast.10, f32[128,128]{1,0:T(8,128)} %fr_hbm.1, ...), custom_call_target="tpu_custom_call" | custom-call | flops 20971520 | bytes 7864320 | tf_op jit(solution)/shard_map/pallas_call | solution.py:497
  14.9 2.0 %shard_map.95 = (f32[2048,128]{1,0:T(8,128)}, f32[2048,128]{1,0:T(8,128)}, f32[2048,128]{1,0:T(8,128)}) custom-call(f32[2048,128]{1,0:T(8,128)S(1)} %get-tuple-element.10.tn, f32[2048,128]{1,0:T(8,128)S(1)} %get-tuple-element.11.un, f32[2048,128]{1,0:T(8,128)S(1)} %get-tuple-element.12.vn, f32[128,128]{1,0:T(8,128)S(1)} %get-tuple-element.13.fix), custom_call_target="tpu_custom_call" | custom-call | tf_op jit(solution)/shard_map/pallas_call | solution.py:527

commit v6 on v5

--- a/solution.py
+++ b/solution.py
@@ -17,7 +17,7 @@
 PG = 0.25 * 0.05
 WEST, EAST, SOUTH, NORTH = 0, 1, 2, 3
 SW, SE, NW, NE = 0, 1, 2, 3
-MSG = 5 * NK + 8
+MSG = 5 * NK
 CHUNK = 4
 
 
@@ -35,9 +35,7 @@
 
 def mirrored(x):
     lane = lax.broadcasted_iota(jnp.int32, x.shape, 1)
-    for bit in (1, 2, 4, 8, 16, 32, 64):
-        x = jnp.where((lane & bit) == 0, pltpu.roll(x, N - bit, 1), pltpu.roll(x, bit, 1))
-    return x
+    return jnp.take_along_axis(x, N - 1 - lane, axis=1)
 
 
 def running_sum(x):
@@ -49,10 +47,10 @@
 
 def kernel(
     n_lon, n_lat,
-    t_hbm, u_hbm, v_hbm, k_hbm, fr_hbm, ind_hbm, str_hbm,
+    t_hbm, u_hbm, v_hbm, k_hbm, t_rows, u_rows, v_rows, k_rows, fr_hbm, ind_hbm, str_hbm,
     tn, un, vn, fix_out,
     t, u, v, kd, p, fa, fb, fr, ind, strata, dep, dep_e, dep_n, cor, fr_e,
-    ue, cols, fix, send, recv, csend, crecv,
+    ue, slabs, cols, fix, send, recv, csend, crecv,
     in_sem, send_sem, recv_sem, csend_sem, crecv_sem,
 ):
     lon, lat = lax.axis_index("lon"), lax.axis_index("lat")
@@ -78,6 +76,11 @@
         for i, (src, dst) in enumerate(
             (
                 (ind_hbm, ind), (str_hbm, strata), (fr_hbm, fr),
+                *(
+                    (ref.at[:, pl.ds(side * (N - 8), 8), :], slabs.at[2 * f + side])
+                    for f, ref in enumerate((t_rows, u_rows, v_rows, k_rows))
+                    for side in (0, 1)
+                ),
                 (t_hbm, t.at[pl.ds(0, FLAT)]), (u_hbm, u.at[pl.ds(0, FLAT)]),
                 (k_hbm, kd.at[pl.ds(0, FLAT)]), (v_hbm, v.at[pl.ds(0, FLAT)]),
             )
@@ -120,8 +123,8 @@
     @pl.when(is_bottom)
     def _():
         recv[SOUTH] = jnp.zeros((MSG, N), jnp.float32)
-        crecv[SW] = jnp.zeros((NK, N), jnp.float32)
-        crecv[SE] = jnp.zeros((NK, N), jnp.float32)
+        crecv[SW] = zero8
+        crecv[SE] = zero8
 
     def set_cor(b, _):
         rows = pl.ds(pl.multiple_of(b * 8, 8), 8)
@@ -184,13 +187,14 @@
         t_c, u_c, k_c, v_c = (column(f, entry) for f in range(4))
         return t_c, u_c, v_c, k_c, plane_column(0, entry)
 
-    def row(ref, j):
-        return ref[pl.ds(j, NK, stride=N), :]
+    slab_rows = slabs.reshape(8 * NK * 8, N)
 
     def edge_rows(j):
-        return (
-            row(t, j), row(u, j), row(v, j), row(kd, j), wide(dep[pl.ds(j, 1), :]),
+        side = 0 if j < 8 else 1
+        t_r, u_r, v_r, k_r = (
+            slab_rows[pl.ds((2 * f + side) * NK * 8 + j % 8, NK, stride=8), :] for f in range(4)
         )
+        return t_r, u_r, v_r, k_r + k_r, wide(dep[pl.ds(j, 1), :])
 
     def x_face(a, b):
         return face(level, jnp.minimum(a[4], b[4]), a[1], b[1], a[0], b[0], a[3], b[3])
@@ -209,23 +213,24 @@
         total = through + (west_of(flow) - flow) + (above - pltpu.roll(above, 1, 0))
         return jnp.where(level < d, tc + SCALE * total, 0.0)
 
+    def marked(values):
+        return (*values[:3], jnp.where(level < values[4], values[3], 0.0))
+
     def stage(side, values, tracer):
-        for f in range(4):
-            send[side, pl.ds(f * NK, NK), :] = values[f]
-        send[side, pl.ds(4 * NK, NK), :] = tracer
-        send[side, pl.ds(5 * NK, 8), :] = values[4][:8]
+        for f, x in enumerate((*marked(values), tracer)):
+            send[side, pl.ds(f * NK, NK), :] = x
 
     def stage_corners(slab, values):
-        x = jnp.zeros((NK, N), jnp.float32)
-        for f in range(5):
-            x = jnp.where(lane == f, pltpu.roll(values[f], f, 1) if f else values[f], x)
-            x = jnp.where(lane == 8 + f, pltpu.roll(values[f], 9 + f, 1), x)
+        x = zero8
+        for f, y in enumerate(marked(values)):
+            for half in (0, 1):
+                z, to = y[8 * half : 8 * half + 8], f + 16 * half
+                x = jnp.where(lane8 == to, pltpu.roll(z, to, 1) if to else z, x)
+                x = jnp.where(lane8 == 8 + to, pltpu.roll(z, 9 + to, 1), x)
         csend[slab] = x
 
-    for f, ref in enumerate((t, u, kd)):
-        loads[3 + f].wait()
-        pack(ref, f, ref is kd)
-    loads[6].wait()
+    for load in loads[3:11]:
+        load.wait()
     r_n, r_s = edge_rows(N - 1), edge_rows(0)
     stage(NORTH, r_n, closed_step(r_n, y_face(edge_rows(N - 2), r_n), x_face))
     stage(SOUTH, r_s, closed_step(r_s, -y_face(r_s, edge_rows(1)), x_face))
@@ -263,8 +268,14 @@
 
     ahead = lax.rem(lon, n_lon // 2) < 3 * n_lon // 16
 
+    def pack_fields():
+        for f, ref in enumerate((t, u, kd, v)):
+            loads[11 + f].wait()
+            pack(ref, f, ref is kd)
+
     @pl.when(ahead)
     def _():
+        pack_fields()
         lax.fori_loop(0, N // 8, tracer, 0, unroll=2)
 
     pl.semaphore_wait(
@@ -307,7 +318,10 @@
         to_se.start()
         to_sw.start()
 
-    pack(v, 3, False)
+    @pl.when(jnp.logical_not(ahead))
+    def _():
+        pack_fields()
+
     c_e, c_w = columns(1), columns(2)
     stage(EAST, c_e, closed_step(c_e, x_face(columns(0), c_e), y_face))
     stage(WEST, c_w, closed_step(c_w, -x_face(c_w, columns(3)), y_face))
@@ -377,18 +391,29 @@
         x = mirrored(recv[NORTH])
         r = lax.broadcasted_iota(jnp.int32, (MSG, N), 0)
         recv[NORTH] = jnp.where((r >= NK) & (r < 3 * NK), -x, x)
-        x = pltpu.roll(crecv[NW], 8, 1)
-        crecv[NW] = jnp.where((lane == 9) | (lane == 10), -x, x)
-        x = pltpu.roll(crecv[NE], N - 8, 1)
-        crecv[NE] = jnp.where((lane == 1) | (lane == 2), -x, x)
+        turned = ((lane8 & 7) == 1) | ((lane8 & 7) == 2)
+        x = crecv[NW]
+        x = pltpu.roll(jnp.where(turned, -x, x), 8, 1)
+        crecv[NW] = x
+        x = crecv[NE]
+        crecv[NE] = pltpu.roll(jnp.where(turned, -x, x), N - 8, 1)
+
+    def with_depth(t_g, u_g, v_g, k_g):
+        return t_g, u_g, v_g, k_g, jnp.where(k_g > 0.0, float(NK), 0.0)
 
     def ghost(slot):
-        parts = [recv[slot, pl.ds(f * NK, NK), :] for f in range(4)]
-        return (*parts, wide(recv[slot, pl.ds(5 * NK, 1), :]))
+        return with_depth(*(recv[slot, pl.ds(f * NK, NK), :] for f in range(4)))
 
     def beyond(slot, entry, to):
         x = crecv[slot]
-        return tuple(pltpu.roll(x, (to - entry - f) % N, 1) for f in range(5))
+
+        def value(f):
+            shift = to - entry - f + N
+            return jnp.concatenate(
+                [pltpu.roll(x, shift % N, 1), pltpu.roll(x, (shift - 16) % N, 1)], 0
+            )
+
+        return with_depth(*(value(f) for f in range(4)))
 
     g_w, g_e, g_s, g_n = ghost(WEST), ghost(EAST), ghost(SOUTH), ghost(NORTH)
     f_w, f_e = x_face(g_w, c_w), x_face(c_e, g_e)
@@ -497,7 +522,7 @@
         outs = pl.pallas_call(
             functools.partial(kernel, n_lon, n_lat),
             out_shape=[*[pltpu.VMEM((FLAT, N), f32)] * 3, pltpu.VMEM((N, N), f32)],
-            in_specs=[pl.BlockSpec(memory_space=pltpu.HBM)] * 7,
+            in_specs=[pl.BlockSpec(memory_space=pltpu.HBM)] * 11,
             out_specs=[pl.BlockSpec(memory_space=pltpu.VMEM)] * 4,
             scratch_shapes=[
                 *[pltpu.VMEM((FLAT + 8, N), f32)] * 4,
@@ -508,13 +533,14 @@
                 pltpu.VMEM((N + 8, N), f32),
                 *[pltpu.VMEM((N, N), f32)] * 4,
                 pltpu.VMEM((FLAT, N), f32),
+                pltpu.VMEM((8, NK, 8, N), f32),
                 pltpu.VMEM(((4 * NK + 2) * 16, N), f32),
                 pltpu.VMEM((N, N), f32),
                 pltpu.VMEM((4, MSG, N), f32),
                 pltpu.VMEM((4, MSG, N), f32),
-                pltpu.VMEM((4, NK, N), f32),
-                pltpu.VMEM((4, NK, N), f32),
-                pltpu.SemaphoreType.DMA((7,)),
+                pltpu.VMEM((2, 8, N), f32),
+                pltpu.VMEM((4, 8, N), f32),
+                pltpu.SemaphoreType.DMA((15,)),
                 *[pltpu.SemaphoreType.DMA((4,))] * 4,
             ],
             compiler_params=pltpu.CompilerParams(
@@ -523,7 +549,7 @@
             cost_estimate=pl.CostEstimate(
                 flops=80 * FLAT * N, bytes_accessed=30 * FLAT * N, transcendentals=0
             ),
-        )(*flat, fr, ind, strata)
+        )(*flat, t, u, v, kd, fr, ind, strata)
         outs = pl.pallas_call(
             finish,
             out_shape=[jax.ShapeDtypeStruct((FLAT, N), f32)] * 3,

time: 17 us -> 17.1 us (level)
  no operation moved by 1% of the time
where the time goes in v6:
time: 17.1 us; the launch traced here: 17 us
  Pallas kernels  16.3 us (95%)
  between operations  0.64 us (4%)
    pallas_call x1, Pallas kernels, on_device(): pl.pallas_call(functools.partial(kernel, n_lon, n_lat), out_shape=[*[pltp...  14.4 us
    pallas_call x1, Pallas kernels, on_device(): pl.pallas_call(finish, out_shape=[jax.ShapeDtypeStruct((FLAT, N), f32)] *...  1.98 us

profile of v6, /device:TPU:7, one launch (start us, length us, event | category | flops | bytes accessed | tf_op | source)
XLA Modules:
  0.0 17.0 jit_solution(15974273152952965395)
XLA Ops:
  0.6 14.4 %shard_map.94 = (f32[2048,128]{1,0:T(8,128)S(1)}, f32[2048,128]{1,0:T(8,128)S(1)}, f32[2048,128]{1,0:T(8,128)S(1)}, f32[128,128]{1,0:T(8,128)S(1)}) custom-call(f32[2048,128]{1,0:T(8,128)} %bitcast.7, f32[2048,128]{1,0:T(8,128)} %bitcast.8, f32[2048,128]{1,0:T(8,128)} %bitcast.9, f32[2048,128]{1,0:T(8,128)} %bitcast.10, f32[16,128,128]{2,1,0:T(8,128)} %t_rows.1, ...), custom_call_target="tpu_custom_call" | custom-call | flops 20971520 | bytes 7864320 | tf_op jit(solution)/shard_map/pallas_call | solution.py:522
  15.0 2.0 %shard_map.95 = (f32[2048,128]{1,0:T(8,128)}, f32[2048,128]{1,0:T(8,128)}, f32[2048,128]{1,0:T(8,128)}) custom-call(f32[2048,128]{1,0:T(8,128)S(1)} %get-tuple-element.10.tn, f32[2048,128]{1,0:T(8,128)S(1)} %get-tuple-element.11.un, f32[2048,128]{1,0:T(8,128)S(1)} %get-tuple-element.12.vn, f32[128,128]{1,0:T(8,128)S(1)} %get-tuple-element.13.fix), custom_call_target="tpu_custom_call" | custom-call | tf_op jit(solution)/shard_map/pallas_call | solution.py:553

commit v7 on v6

--- a/solution.py
+++ b/solution.py
@@ -51,7 +51,7 @@
     tn, un, vn, fix_out,
     t, u, v, kd, p, fa, fb, fr, ind, strata, dep, dep_e, dep_n, cor, fr_e,
     ue, slabs, cols, fix, send, recv, csend, crecv,
-    in_sem, send_sem, recv_sem, csend_sem, crecv_sem,
+    in_sem, send_sem, recv_sem, csend_sem, crecv_sem, ready,
 ):
     lon, lat = lax.axis_index("lon"), lax.axis_index("lat")
     is_top, is_bottom = lat == n_lat - 1, lat == 0
@@ -90,24 +90,31 @@
         load.start()
     barrier = pltpu.get_barrier_semaphore()
 
-    def greet(place):
-        pl.semaphore_signal(barrier, inc=1, device_id=at(place), device_id_type=MESH)
-
-    for place in (west, east, north):
-        greet(place)
-
-    @pl.when(not_own_e)
-    def _():
-        greet(north_e)
-
-    @pl.when(not_own_w)
-    def _():
-        greet(north_w)
-
-    @pl.when(not_bottom)
-    def _():
-        for place in (south, south_e, south_w):
-            greet(place)
+    def is_early(place):
+        return lax.rem(place[1], n_lon // 2) < n_lon // 4
+
+    early = is_early((lat, lon))
+    always = lat >= 0
+    peers = (
+        (east, always, 1),
+        (west, always, 0),
+        (north, always, jnp.where(is_top, 2, 3)),
+        (south, not_bottom, 2),
+        (north_e, not_own_e, jnp.where(is_top, 4, 7)),
+        (north_w, not_own_w, jnp.where(is_top, 5, 6)),
+        (south_e, not_bottom, 5),
+        (south_w, not_bottom, 4),
+    )
+    to_late = [ok & early & jnp.logical_not(is_early(place)) for place, ok, _ in peers]
+    to_early = [ok & jnp.logical_not(early) & is_early(place) for place, ok, _ in peers]
+    expected = jnp.int32(0)
+    for (place, ok, _), ahead, behind in zip(peers, to_early, to_late):
+
+        @pl.when(ok & jnp.logical_not(ahead))
+        def _(place=place):
+            pl.semaphore_signal(barrier, inc=1, device_id=at(place), device_id_type=MESH)
+
+        expected = expected + (ok & jnp.logical_not(behind)).astype(jnp.int32)
 
     lane8 = lax.broadcasted_iota(jnp.int32, (8, N), 1)
     zero8 = jnp.zeros((8, N), jnp.float32)
@@ -266,22 +273,19 @@
             p[pl.ds(r + k * PAD + 8, 8), :] = press
         return 0
 
-    ahead = lax.rem(lon, n_lon // 2) < 3 * n_lon // 16
-
     def pack_fields():
         for f, ref in enumerate((t, u, kd, v)):
             loads[11 + f].wait()
             pack(ref, f, ref is kd)
 
-    @pl.when(ahead)
-    def _():
-        pack_fields()
-        lax.fori_loop(0, N // 8, tracer, 0, unroll=2)
-
-    pl.semaphore_wait(
-        barrier,
-        jnp.where(is_bottom, 5, 8) - own_e.astype(jnp.int32) - own_w.astype(jnp.int32),
-    )
+    pl.semaphore_wait(barrier, expected)
+    for (place, _, number), ahead in zip(peers, to_early):
+
+        @pl.when(ahead)
+        def _(place=place, number=number):
+            pl.semaphore_signal(
+                ready.at[number], inc=1, device_id=at(place), device_id_type=MESH
+            )
 
     def rim(side, slot, place):
         return pltpu.make_async_remote_copy(
@@ -302,35 +306,19 @@
     to_nw = corner(0, 1, jnp.where(is_top, NW, SE), north_w)
     to_se, to_sw = corner(1, 2, NW, south_e), corner(1, 3, NE, south_w)
 
-    to_north.start()
-
-    @pl.when(not_own_e)
-    def _():
-        to_ne.start()
-
-    @pl.when(not_own_w)
-    def _():
-        to_nw.start()
-
-    @pl.when(not_bottom)
-    def _():
-        to_south.start()
-        to_se.start()
-        to_sw.start()
-
-    @pl.when(jnp.logical_not(ahead))
-    def _():
-        pack_fields()
-
+    messages = (to_east, to_west, to_north, to_south, to_ne, to_nw, to_se, to_sw)
+
+    def start(numbers):
+        for i in numbers:
+            pl.when(peers[i][1] & jnp.logical_not(to_late[i]))(messages[i].start)
+
+    start((2, 3, 4, 5, 6, 7))
+    pack_fields()
     c_e, c_w = columns(1), columns(2)
     stage(EAST, c_e, closed_step(c_e, x_face(columns(0), c_e), y_face))
     stage(WEST, c_w, closed_step(c_w, -x_face(c_w, columns(3)), y_face))
-    to_east.start()
-    to_west.start()
-
-    @pl.when(jnp.logical_not(ahead))
-    def _():
-        lax.fori_loop(0, N // 8, tracer, 0, unroll=2)
+    start((0, 1))
+    lax.fori_loop(0, N // 8, tracer, 0, unroll=2)
 
     def momentum(b, _):
         r = pl.multiple_of(b * 8, 8)
@@ -360,6 +348,13 @@
 
     lax.fori_loop(0, N // 8, momentum, 0)
 
+    for i, message in enumerate(messages):
+
+        @pl.when(to_late[i])
+        def _(i=i, message=message):
+            pl.semaphore_wait(ready.at[i], 1)
+            message.start()
+
     rim(NORTH, NORTH, north).wait_recv()
     rim(EAST, EAST, east).wait_recv()
     rim(WEST, WEST, west).wait_recv()
@@ -466,23 +461,8 @@
     fix[pl.ds(97, NK, stride=2), :] = t_w
     fix_out[...] = fix[...].T
 
-    to_north.wait_send()
-    to_east.wait_send()
-    to_west.wait_send()
-
-    @pl.when(not_own_e)
-    def _():
-        to_ne.wait_send()
-
-    @pl.when(not_own_w)
-    def _():
-        to_nw.wait_send()
-
-    @pl.when(not_bottom)
-    def _():
-        to_south.wait_send()
-        to_se.wait_send()
-        to_sw.wait_send()
+    for (_, ok, _), message in zip(peers, messages):
+        pl.when(ok)(message.wait_send)
 
 
 def finish(tn, un, vn, fix, t_out, u_out, v_out, t, u, v, out_sem):
@@ -542,6 +522,7 @@
                 pltpu.VMEM((4, 8, N), f32),
                 pltpu.SemaphoreType.DMA((15,)),
                 *[pltpu.SemaphoreType.DMA((4,))] * 4,
+                pltpu.SemaphoreType.REGULAR((8,)),
             ],
             compiler_params=pltpu.CompilerParams(
                 collective_id=0, has_side_effects=True, vmem_limit_bytes=60 * 1024 * 1024

time: 17.1 us -> 18.3 us (1.070)
  the two profiles are of different devices: /device:TPU:7 before, /device:TPU:134 now
where the time goes in v7:
time: 18.3 us; the launch traced here: 18.2 us
  Pallas kernels  17.5 us (96%)
  between operations  0.64 us (3%)
    pallas_call x1, Pallas kernels, on_device(): pl.pallas_call(functools.partial(kernel, n_lon, n_lat), out_shape=[*[pltp...  15.6 us
    pallas_call x1, Pallas kernels, on_device(): pl.pallas_call(finish, out_shape=[jax.ShapeDtypeStruct((FLAT, N), f32)] *...  1.98 us

profile of v7, /device:TPU:134, one launch (start us, length us, event | category | flops | bytes accessed | tf_op | source)
XLA Modules:
  0.0 18.2 jit_solution(15231448196741045694)
XLA Ops:
  0.6 15.6 %shard_map.94 = (f32[2048,128]{1,0:T(8,128)S(1)}, f32[2048,128]{1,0:T(8,128)S(1)}, f32[2048,128]{1,0:T(8,128)S(1)}, f32[128,128]{1,0:T(8,128)S(1)}) custom-call(f32[2048,128]{1,0:T(8,128)} %bitcast.7, f32[2048,128]{1,0:T(8,128)} %bitcast.8, f32[2048,128]{1,0:T(8,128)} %bitcast.9, f32[2048,128]{1,0:T(8,128)} %bitcast.10, f32[16,128,128]{2,1,0:T(8,128)} %t_rows.1, ...), custom_call_target="tpu_custom_call" | custom-call | flops 20971520 | bytes 7864320 | tf_op jit(solution)/shard_map/pallas_call | solution.py:502
  16.2 2.0 %shard_map.95 = (f32[2048,128]{1,0:T(8,128)}, f32[2048,128]{1,0:T(8,128)}, f32[2048,128]{1,0:T(8,128)}) custom-call(f32[2048,128]{1,0:T(8,128)S(1)} %get-tuple-element.10.tn, f32[2048,128]{1,0:T(8,128)S(1)} %get-tuple-element.11.un, f32[2048,128]{1,0:T(8,128)S(1)} %get-tuple-element.12.vn, f32[128,128]{1,0:T(8,128)S(1)} %get-tuple-element.13.fix), custom_call_target="tpu_custom_call" | custom-call | tf_op jit(solution)/shard_map/pallas_call | solution.py:534

commit v8 on v7

--- a/solution.py
+++ b/solution.py
@@ -320,6 +320,13 @@
     start((0, 1))
     lax.fori_loop(0, N // 8, tracer, 0, unroll=2)
 
+    for i, message in enumerate(messages):
+
+        @pl.when(to_late[i])
+        def _(i=i, message=message):
+            pl.semaphore_wait(ready.at[i], 1)
+            message.start()
+
     def momentum(b, _):
         r = pl.multiple_of(b * 8, 8)
         rows = pl.ds(r, 8)
@@ -347,13 +354,6 @@
         return 0
 
     lax.fori_loop(0, N // 8, momentum, 0)
-
-    for i, message in enumerate(messages):
-
-        @pl.when(to_late[i])
-        def _(i=i, message=message):
-            pl.semaphore_wait(ready.at[i], 1)
-            message.start()
 
     rim(NORTH, NORTH, north).wait_recv()
     rim(EAST, EAST, east).wait_recv()

time: 18.3 us -> 16.8 us (0.918)
  the two profiles are of different devices: /device:TPU:134 before, /device:TPU:6 now
where the time goes in v8:
time: 16.8 us; the launch traced here: 16.7 us
  Pallas kernels  16 us (95%)
  between operations  0.64 us (4%)
    pallas_call x1, Pallas kernels, on_device(): pl.pallas_call(functools.partial(kernel, n_lon, n_lat), out_shape=[*[pltp...  14 us
    pallas_call x1, Pallas kernels, on_device(): pl.pallas_call(finish, out_shape=[jax.ShapeDtypeStruct((FLAT, N), f32)] *...  1.98 us

profile of v8, /device:TPU:6, one launch (start us, length us, event | category | flops | bytes accessed | tf_op | source)
XLA Modules:
  0.0 16.7 jit_solution(6935279416615525016)
XLA Ops:
  0.6 14.0 %shard_map.94 = (f32[2048,128]{1,0:T(8,128)S(1)}, f32[2048,128]{1,0:T(8,128)S(1)}, f32[2048,128]{1,0:T(8,128)S(1)}, f32[128,128]{1,0:T(8,128)S(1)}) custom-call(f32[2048,128]{1,0:T(8,128)} %bitcast.7, f32[2048,128]{1,0:T(8,128)} %bitcast.8, f32[2048,128]{1,0:T(8,128)} %bitcast.9, f32[2048,128]{1,0:T(8,128)} %bitcast.10, f32[16,128,128]{2,1,0:T(8,128)} %t_rows.1, ...), custom_call_target="tpu_custom_call" | custom-call | flops 20971520 | bytes 7864320 | tf_op jit(solution)/shard_map/pallas_call | solution.py:502
  14.7 2.0 %shard_map.95 = (f32[2048,128]{1,0:T(8,128)}, f32[2048,128]{1,0:T(8,128)}, f32[2048,128]{1,0:T(8,128)}) custom-call(f32[2048,128]{1,0:T(8,128)S(1)} %get-tuple-element.10.tn, f32[2048,128]{1,0:T(8,128)S(1)} %get-tuple-element.11.un, f32[2048,128]{1,0:T(8,128)S(1)} %get-tuple-element.12.vn, f32[128,128]{1,0:T(8,128)S(1)} %get-tuple-element.13.fix), custom_call_target="tpu_custom_call" | custom-call | tf_op jit(solution)/shard_map/pallas_call | solution.py:534

commit v9 on v8

--- a/solution.py
+++ b/solution.py
@@ -75,18 +75,19 @@
         pltpu.make_async_copy(src, dst, in_sem.at[i])
         for i, (src, dst) in enumerate(
             (
-                (ind_hbm, ind), (str_hbm, strata), (fr_hbm, fr),
+                (ind_hbm, ind), (str_hbm, strata),
                 *(
                     (ref.at[:, pl.ds(side * (N - 8), 8), :], slabs.at[2 * f + side])
                     for f, ref in enumerate((t_rows, u_rows, v_rows, k_rows))
                     for side in (0, 1)
                 ),
+                (fr_hbm, fr),
                 (t_hbm, t.at[pl.ds(0, FLAT)]), (u_hbm, u.at[pl.ds(0, FLAT)]),
                 (k_hbm, kd.at[pl.ds(0, FLAT)]), (v_hbm, v.at[pl.ds(0, FLAT)]),
             )
         )
     ]
-    for load in loads:
+    for load in loads[:10]:
         load.start()
     barrier = pltpu.get_barrier_semaphore()
 
@@ -116,57 +117,24 @@
 
         expected = expected + (ok & jnp.logical_not(behind)).astype(jnp.int32)
 
+    for load in loads[10:]:
+        load.start()
+
     lane8 = lax.broadcasted_iota(jnp.int32, (8, N), 1)
     zero8 = jnp.zeros((8, N), jnp.float32)
     lane = lax.broadcasted_iota(jnp.int32, (NK, N), 1)
     level = lax.broadcasted_iota(jnp.int32, (NK, N), 0).astype(jnp.float32)
     first, last = lane == 0, lane == N - 1
 
-    for k in range(NK + 1):
-        p[pl.ds(k * PAD, 8), :] = zero8
-        fa[pl.ds(k * PAD, 8), :] = zero8
-        fb[pl.ds(k * PAD, 8), :] = zero8
-
-    @pl.when(is_bottom)
-    def _():
-        recv[SOUTH] = jnp.zeros((MSG, N), jnp.float32)
-        crecv[SW] = zero8
-        crecv[SE] = zero8
-
-    def set_cor(b, _):
-        rows = pl.ds(pl.multiple_of(b * 8, 8), 8)
-        j = lax.broadcasted_iota(jnp.int32, (8, N), 0) + (b * 8 + lat * N)
-        cor[rows, :] = 0.25 * jnp.sin(
-            jnp.pi * ((j.astype(jnp.float32) + 0.5) / (N * n_lat) - 0.5)
-        )
-        return 0
-
-    lax.fori_loop(0, N // 8, set_cor, 0)
-
-    for load in loads[:3]:
+    for load in loads[:2]:
         load.wait()
     dep[pl.ds(N, 8), :] = zero8
     dep[pl.ds(0, N), :] = (ind[...] * strata[...]).astype(jnp.float32)
-    fr[...] = fr[...] * 0.25
-
-    def set_depth(b, _):
-        r = pl.multiple_of(b * 8, 8)
-        rows = pl.ds(r, 8)
-        d = dep[rows, :]
-        dep_e[rows, :] = jnp.where(lane8 == N - 1, 0.0, jnp.minimum(d, east_of(d)))
-        dep_n[rows, :] = jnp.minimum(d, dep[pl.ds(r + 1, 8), :])
-        fr_e[rows, :] = east_of(fr[rows, :])
-        return 0
-
-    lax.fori_loop(0, N // 8, set_depth, 0, unroll=True)
 
     def set_columns(place, x):
         y = x.T
         cols[pl.ds(place * 16, 8), :] = y[N - 8 :]
         cols[pl.ds(place * 16 + 8, 8), :] = y[:8]
-
-    set_columns(4 * NK, dep[pl.ds(0, N), :])
-    set_columns(4 * NK + 1, fr[...])
 
     def pack(ref, f, double):
         def step(k, _):
@@ -236,7 +204,7 @@
                 x = jnp.where(lane8 == 8 + to, pltpu.roll(z, 9 + to, 1), x)
         csend[slab] = x
 
-    for load in loads[3:11]:
+    for load in loads[2:10]:
         load.wait()
     r_n, r_s = edge_rows(N - 1), edge_rows(0)
     stage(NORTH, r_n, closed_step(r_n, y_face(edge_rows(N - 2), r_n), x_face))
@@ -279,14 +247,6 @@
             pack(ref, f, ref is kd)
 
     pl.semaphore_wait(barrier, expected)
-    for (place, _, number), ahead in zip(peers, to_early):
-
-        @pl.when(ahead)
-        def _(place=place, number=number):
-            pl.semaphore_signal(
-                ready.at[number], inc=1, device_id=at(place), device_id_type=MESH
-            )
-
     def rim(side, slot, place):
         return pltpu.make_async_remote_copy(
             src_ref=send.at[side], dst_ref=recv.at[slot], send_sem=send_sem.at[side],
@@ -313,6 +273,52 @@
             pl.when(peers[i][1] & jnp.logical_not(to_late[i]))(messages[i].start)
 
     start((2, 3, 4, 5, 6, 7))
+    for (place, _, number), ahead in zip(peers, to_early):
+
+        @pl.when(ahead)
+        def _(place=place, number=number):
+            pl.semaphore_signal(
+                ready.at[number], inc=1, device_id=at(place), device_id_type=MESH
+            )
+
+    for k in range(NK + 1):
+        p[pl.ds(k * PAD, 8), :] = zero8
+        fa[pl.ds(k * PAD, 8), :] = zero8
+        fb[pl.ds(k * PAD, 8), :] = zero8
+
+    @pl.when(is_bottom)
+    def _():
+        recv[SOUTH] = jnp.zeros((MSG, N), jnp.float32)
+        crecv[SW] = zero8
+        crecv[SE] = zero8
+
+    def set_cor(b, _):
+        rows = pl.ds(pl.multiple_of(b * 8, 8), 8)
+        j = lax.broadcasted_iota(jnp.int32, (8, N), 0) + (b * 8 + lat * N)
+        cor[rows, :] = 0.25 * jnp.sin(
+            jnp.pi * ((j.astype(jnp.float32) + 0.5) / (N * n_lat) - 0.5)
+        )
+        return 0
+
+    lax.fori_loop(0, N // 8, set_cor, 0)
+
+    loads[10].wait()
+    fr[...] = fr[...] * 0.25
+
+    def set_depth(b, _):
+        r = pl.multiple_of(b * 8, 8)
+        rows = pl.ds(r, 8)
+        d = dep[rows, :]
+        dep_e[rows, :] = jnp.where(lane8 == N - 1, 0.0, jnp.minimum(d, east_of(d)))
+        dep_n[rows, :] = jnp.minimum(d, dep[pl.ds(r + 1, 8), :])
+        fr_e[rows, :] = east_of(fr[rows, :])
+        return 0
+
+    lax.fori_loop(0, N // 8, set_depth, 0, unroll=True)
+
+    set_columns(4 * NK, dep[pl.ds(0, N), :])
+    set_columns(4 * NK + 1, fr[...])
+
     pack_fields()
     c_e, c_w = columns(1), columns(2)
     stage(EAST, c_e, closed_step(c_e, x_face(columns(0), c_e), y_face))

time: 16.8 us -> 17.6 us (1.048)
  the two profiles are of different devices: /device:TPU:6 before, /device:TPU:1 now
where the time goes in v9:
time: 17.6 us; the launch traced here: 17.5 us
  Pallas kernels  16.9 us (96%)
  between operations  0.64 us (4%)
    pallas_call x1, Pallas kernels, on_device(): pl.pallas_call(functools.partial(kernel, n_lon, n_lat), out_shape=[*[pltp...  14.9 us
    pallas_call x1, Pallas kernels, on_device(): pl.pallas_call(finish, out_shape=[jax.ShapeDtypeStruct((FLAT, N), f32)] *...  1.98 us

profile of v9, /device:TPU:1, one launch (start us, length us, event | category | flops | bytes accessed | tf_op | source)
XLA Modules:
  0.0 17.5 jit_solution(15245961459732653150)
XLA Ops:
  0.6 14.9 %shard_map.94 = (f32[2048,128]{1,0:T(8,128)S(1)}, f32[2048,128]{1,0:T(8,128)S(1)}, f32[2048,128]{1,0:T(8,128)S(1)}, f32[128,128]{1,0:T(8,128)S(1)}) custom-call(f32[2048,128]{1,0:T(8,128)} %bitcast.7, f32[2048,128]{1,0:T(8,128)} %bitcast.8, f32[2048,128]{1,0:T(8,128)} %bitcast.9, f32[2048,128]{1,0:T(8,128)} %bitcast.10, f32[16,128,128]{2,1,0:T(8,128)} %t_rows.1, ...), custom_call_target="tpu_custom_call" | custom-call | flops 20971520 | bytes 7864320 | tf_op jit(solution)/shard_map/pallas_call | solution.py:508
  15.5 2.0 %shard_map.95 = (f32[2048,128]{1,0:T(8,128)}, f32[2048,128]{1,0:T(8,128)}, f32[2048,128]{1,0:T(8,128)}) custom-call(f32[2048,128]{1,0:T(8,128)S(1)} %get-tuple-element.10.tn, f32[2048,128]{1,0:T(8,128)S(1)} %get-tuple-element.11.un, f32[2048,128]{1,0:T(8,128)S(1)} %get-tuple-element.12.vn, f32[128,128]{1,0:T(8,128)S(1)} %get-tuple-element.13.fix), custom_call_target="tpu_custom_call" | custom-call | tf_op jit(solution)/shard_map/pallas_call | solution.py:540
